TPU v7x, 32 devices: a whole 2x2x4 slice. The times are simulated.
32 devices in a mesh: dp: 2 (over core), blk: 8 (over z, x), head: 2 (over y).
Axes of the slice: x: 2, y: 2, z: 4, core: 2. Of those that a mesh axis runs over, the one named last changes fastest.
Arguments:
- queries: bfloat16 [8192, 5120], P(('dp', 'blk'), 'head'), parts along dimension 0, may hold values from -20 to 20, as said below
- keys: bfloat16 [8192, 5120], P(('dp', 'blk'), 'head'), parts along dimension 0, may hold values from -20 to 20
- values: bfloat16 [8192, 5120], P(('dp', 'blk'), 'head'), parts along dimension 0, may hold values from -6 to 6
- block_list: int32 [64, 16], P(('dp', 'blk')), parts along dimension 0, may hold values from 0 to 31, as said below
- block_count: int32 [64], P(('dp', 'blk')), parts along dimension 0, may hold values from 4 to 16, as said below
- out_weight: bfloat16 [5120, 5120], P('head'), may hold values from -0.25 to 0.25
Outputs:
- projected: bfloat16 [8192, 5120], P(('dp', 'blk', 'head')), parts along dimension 0
There are 2 independent parts, one for each index of `dp`. A program takes and returns all parts, laid end to end along the dimension named above; an argument that names none is the same for every part. Nothing has to cross between parts.
Inputs may be any that keep to these rules, and one draw needn't show every extreme that they name: `block_list`: each row names 16 different key blocks of the same clip; its first entry is the query block itself; only the first block_count entries of a row are used. `block_count`: some query block uses all 16 entries in every draw. `queries`: query entries lie in the stated range.
All inputs are finite; a program needn't handle non-finite values.
Results may differ from a plain program's by a relative error of at most 0.02.
Values may be sent and summed in bfloat16 or wider, within the bound.
A program may use at most 192 MiB of HBM per device.

v0:
```python
import math

import jax
import jax.numpy as jnp
from jax import lax
from jax.sharding import PartitionSpec as P

HD = 128
BS = 128
KB = 16


def on_device(queries, keys, values, block_list, block_count, out_weight):
    tok_rows, feature_width = queries.shape
    head_count = feature_width // HD
    query_blocks = tok_rows // BS
    block_total = tok_rows * lax.axis_size("blk") // BS
    score_scale = 1.0 / math.sqrt(HD)
    query_heads = queries.reshape(tok_rows, head_count, HD)
    block_range = jnp.arange(block_total, dtype=jnp.int32)
    listed = jnp.arange(KB, dtype=jnp.int32)[None, :] < block_count[:, None]
    matches = listed[:, :, None] & (block_list[:, :, None] == block_range[None, None, :])
    allowed = jnp.sum(jnp.where(matches, 1.0, 0.0), axis=1).astype(jnp.float32)

    def attend(state_in, key_piece, value_piece, row_start):
        running, totals, summed = state_in
        row_count = key_piece.shape[0]
        piece_blocks = (row_start + jnp.arange(row_count, dtype=jnp.int32)) // BS
        onehot = jnp.where(piece_blocks[:, None] == block_range[None, :], 1.0, 0.0).astype(
            jnp.float32
        )
        columns = jnp.einsum("bn,pn->bp", allowed, onehot)
        visible = jnp.broadcast_to(
            columns[:, None, :] > 0.5, (query_blocks, BS, row_count)
        ).reshape(tok_rows, row_count)
        scores = (
            jnp.einsum(
                "qhd,khd->hqk",
                query_heads,
                key_piece.reshape(row_count, head_count, HD),
                preferred_element_type=jnp.float32,
            )
            * score_scale
        )
        scores = jnp.where(visible[None], scores, -jnp.inf)
        highest = jnp.maximum(running, jnp.max(scores, axis=-1))
        weights = jnp.where(visible[None], jnp.exp(scores - highest[:, :, None]), 0.0)
        rescale = jnp.exp(running - highest)
        totals = totals * rescale + jnp.sum(weights, axis=-1)
        update = jnp.einsum(
            "hqk,khd->qhd",
            weights.astype(jnp.bfloat16),
            value_piece.reshape(row_count, head_count, HD),
            preferred_element_type=jnp.float32,
        )
        summed = summed * jnp.transpose(rescale)[:, :, None] + update
        return (highest, totals, summed)

    initial = (
        jnp.full((head_count, tok_rows), -1e30, jnp.float32),
        jnp.zeros((head_count, tok_rows), jnp.float32),
        jnp.zeros((tok_rows, head_count, HD), jnp.float32),
    )
    key_piece = lax.all_gather(keys, "blk", axis=0, tiled=True)
    value_piece = lax.all_gather(values, "blk", axis=0, tiled=True)
    row_count = key_piece.shape[0]
    sub_rows = 512
    key_split = key_piece.reshape(row_count // sub_rows, sub_rows, feature_width)
    value_split = value_piece.reshape(row_count // sub_rows, sub_rows, feature_width)
    offsets = sub_rows * jnp.arange(row_count // sub_rows, dtype=jnp.int32)

    def advance(inner_state, packed):
        key_sub, value_sub, offset_now = packed
        return (attend(inner_state, key_sub, value_sub, offset_now), None)

    finished, unused = lax.scan(advance, initial, (key_split, value_split, offsets))
    running, totals, summed = finished
    attended = (
        (summed / jnp.transpose(totals)[:, :, None])
        .astype(jnp.bfloat16)
        .reshape(tok_rows, feature_width)
    )
    return lax.psum_scatter(
        jnp.dot(attended, out_weight, preferred_element_type=jnp.float32).astype(jnp.bfloat16),
        "head",
        scatter_dimension=0,
        tiled=True,
    )


def solution(mesh):
    placed = (
        P(("dp", "blk"), "head"),
        P(("dp", "blk"), "head"),
        P(("dp", "blk"), "head"),
        P(("dp", "blk"), None),
        P(("dp", "blk")),
        P("head", None),
    )
    return jax.shard_map(
        on_device,
        mesh=mesh,
        in_specs=placed,
        out_specs=P(("dp", "blk", "head"), None),
        check_vma=False,
    )
```

profile of v0, /device:TPU:10, one launch (start us, length us, event | category | flops | bytes accessed | tf_op | source)
XLA Modules:
  0.0 1325.2 jit_solution(18437813999502840299)
XLA Ops:
  13.8 397.1 %all-gather.3.cloned.1.call-done = bf16[4096,2560]{1,0:T(8,128)(2,1)} async-done(((bf16[512,2560]{1,0:T(8,128)(2,1)}), bf16[4096,2560]{1,0:T(8,128)(2,1)}) %all-gather.3.cloned.1.call-update) | async-done | bytes 20971536 | tf_op jit(solution)/shard_map/all_gather | solution.py:64
  411.0 403.3 %all-gather.5.cloned.1.call-done = bf16[4096,2560]{1,0:T(8,128)(2,1)} async-done(((bf16[512,2560]{1,0:T(8,128)(2,1)}), bf16[4096,2560]{1,0:T(8,128)(2,1)}) %all-gather.5.cloned.1.call-update) | async-done | bytes 20971536 | tf_op jit(solution)/shard_map/all_gather | solution.py:65
  814.3 413.9 %while.17 = (s32[]{:T(128)}, f32[20,512]{1,0:T(8,128)S(1)}, f32[20,512]{1,0:T(8,128)S(1)}, f32[512,20,128]{0,2,1:T(8,128)}, s32[8]{0:T(128)S(1)}, /*index=5*/bf1...) while((s32[]{:T(128)}, f32[20,512]{1,0:T(8,128)S(1)}, ...), condition=%wide.region_4.5_spmd.clone, body=%wide.region_1.4_spmd.clone.sunk | while | flops 2756679680 | bytes 104477064 | solution.py:76
  826.6 13.2 fusion.50
  842.5 12.3 bitcast_add_fusion.2
  854.8 9.8 fusion.52
  877.1 13.2 fusion.50
  893.0 13.8 %bitcast_add_fusion.2 = f32[512,20,128]{0,2,1:T(8,128)} fusion(f32[512,20,128]{0,2,1:T(8,128)} %get-tuple-element.298, f32[512,20]{0,1:T(8,128)S(1)} %get-tuple-element.282, pred[]{:T(512)S(6)} %compare.14, bf16[512,20,128]{0,2,1:T(8,128)(2,1)} %bitcast.70, f32[20,512,512]{2,1,0:T(8,128)} %get-tuple-element.281, ...), kind=kOutput, calls=%fused_computation.8.clone.1 | convolution fusion | flops 1372323840 | bytes 34422784 | tf_op jit(solution)/shard_map/while/body/eval_jaxpr/hqk,khd->qhd/dot_general | solution.py:50
  906.7 9.8 fusion.52
  924.6 4.4 copy.42
  929.0 13.2 fusion.50
  944.9 13.8 %bitcast_add_fusion.2 = f32[512,20,128]{0,2,1:T(8,128)} fusion(f32[512,20,128]{0,2,1:T(8,128)} %get-tuple-element.298, f32[512,20]{0,1:T(8,128)S(1)} %get-tuple-element.282, pred[]{:T(512)S(6)} %compare.14, bf16[512,20,128]{0,2,1:T(8,128)(2,1)} %bitcast.70, f32[20,512,512]{2,1,0:T(8,128)} %get-tuple-element.281, ...), kind=kOutput, calls=%fused_computation.8.clone.1 | convolution fusion | flops 1372323840 | bytes 34422784 | tf_op jit(solution)/shard_map/while/body/eval_jaxpr/hqk,khd->qhd/dot_general | solution.py:50
  958.7 9.8 fusion.52
  980.9 13.2 fusion.50
  996.8 13.8 %bitcast_add_fusion.2 = f32[512,20,128]{0,2,1:T(8,128)} fusion(f32[512,20,128]{0,2,1:T(8,128)} %get-tuple-element.298, f32[512,20]{0,1:T(8,128)S(1)} %get-tuple-element.282, pred[]{:T(512)S(6)} %compare.14, bf16[512,20,128]{0,2,1:T(8,128)(2,1)} %bitcast.70, f32[20,512,512]{2,1,0:T(8,128)} %get-tuple-element.281, ...), kind=kOutput, calls=%fused_computation.8.clone.1 | convolution fusion | flops 1372323840 | bytes 34422784 | tf_op jit(solution)/shard_map/while/body/eval_jaxpr/hqk,khd->qhd/dot_general | solution.py:50
  1010.6 9.8 fusion.52
  1028.4 4.4 copy.42
  1032.8 13.2 fusion.50
  1048.7 13.8 %bitcast_add_fusion.2 = f32[512,20,128]{0,2,1:T(8,128)} fusion(f32[512,20,128]{0,2,1:T(8,128)} %get-tuple-element.298, f32[512,20]{0,1:T(8,128)S(1)} %get-tuple-element.282, pred[]{:T(512)S(6)} %compare.14, bf16[512,20,128]{0,2,1:T(8,128)(2,1)} %bitcast.70, f32[20,512,512]{2,1,0:T(8,128)} %get-tuple-element.281, ...), kind=kOutput, calls=%fused_computation.8.clone.1 | convolution fusion | flops 1372323840 | bytes 34422784 | tf_op jit(solution)/shard_map/while/body/eval_jaxpr/hqk,khd->qhd/dot_general | solution.py:50
  1062.5 9.8 fusion.52
  1084.8 13.2 fusion.50
  1100.6 13.8 %bitcast_add_fusion.2 = f32[512,20,128]{0,2,1:T(8,128)} fusion(f32[512,20,128]{0,2,1:T(8,128)} %get-tuple-element.298, f32[512,20]{0,1:T(8,128)S(1)} %get-tuple-element.282, pred[]{:T(512)S(6)} %compare.14, bf16[512,20,128]{0,2,1:T(8,128)(2,1)} %bitcast.70, f32[20,512,512]{2,1,0:T(8,128)} %get-tuple-element.281, ...), kind=kOutput, calls=%fused_computation.8.clone.1 | convolution fusion | flops 1372323840 | bytes 34422784 | tf_op jit(solution)/shard_map/while/body/eval_jaxpr/hqk,khd->qhd/dot_general | solution.py:50
  1114.4 9.8 fusion.52
  1132.3 4.4 copy.42
  1136.7 13.2 fusion.50
  1152.6 13.8 %bitcast_add_fusion.2 = f32[512,20,128]{0,2,1:T(8,128)} fusion(f32[512,20,128]{0,2,1:T(8,128)} %get-tuple-element.298, f32[512,20]{0,1:T(8,128)S(1)} %get-tuple-element.282, pred[]{:T(512)S(6)} %compare.14, bf16[512,20,128]{0,2,1:T(8,128)(2,1)} %bitcast.70, f32[20,512,512]{2,1,0:T(8,128)} %get-tuple-element.281, ...), kind=kOutput, calls=%fused_computation.8.clone.1 | convolution fusion | flops 1372323840 | bytes 34422784 | tf_op jit(solution)/shard_map/while/body/eval_jaxpr/hqk,khd->qhd/dot_general | solution.py:50
  1166.4 9.8 fusion.52
  1188.6 13.2 fusion.50
  1204.5 13.8 %bitcast_add_fusion.2 = f32[512,20,128]{0,2,1:T(8,128)} fusion(f32[512,20,128]{0,2,1:T(8,128)} %get-tuple-element.298, f32[512,20]{0,1:T(8,128)S(1)} %get-tuple-element.282, pred[]{:T(512)S(6)} %compare.14, bf16[512,20,128]{0,2,1:T(8,128)(2,1)} %bitcast.70, f32[20,512,512]{2,1,0:T(8,128)} %get-tuple-element.281, ...), kind=kOutput, calls=%fused_computation.8.clone.1 | convolution fusion | flops 1372323840 | bytes 34422784 | tf_op jit(solution)/shard_map/while/body/eval_jaxpr/hqk,khd->qhd/dot_general | solution.py:50
  1218.3 9.8 fusion.52
  1231.5 20.4 %convolution_convert_fusion = bf16[512,5120]{1,0:T(8,128)(2,1)} fusion(bf16[512,2560]{0,1:T(8,128)(2,1)S(1)} %bitcast.78, bf16[2560,5120]{1,0:T(8,128)(2,1)} %param.13), kind=kOutput, calls=%fused_computation.39 | convolution fusion | flops 13424394240 | bytes 34078720 | tf_op jit(solution)/shard_map/dot_general | solution.py:84
  1251.9 66.8 %reduce-scatter.2.cloned.1.call-done = bf16[256,5120]{1,0:T(8,128)(2,1)} async-done(((bf16[512,5120]{1,0:T(8,128)(2,1)}), bf16[256,5120]{1,0:T(8,128)(2,1)}) %reduce-scatter.2.cloned.1.call-update) | async-done | bytes 2621456 | tf_op jit(solution)/shard_map/reduce_scatter | solution.py:83
  (112 shorter events, 117.4 us)
Async XLA Ops:
  6.5 404.4 %all-gather.3.cloned.1.call-start = ((), (), s32[]{:S(2)}) async-start(), calls=%async_computation.1 | async-start | bytes 23592960 | tf_op jit(solution)/shard_map/all_gather | solution.py:64
  7.3 807.0 %all-gather.5.cloned.1.call-start = ((), (), s32[]{:S(2)}) async-start(), calls=%async_computation.2 | async-start | bytes 23592960 | tf_op jit(solution)/shard_map/all_gather | solution.py:65
  8.0 1310.7 %reduce-scatter.2.cloned.1.call-start = ((), (), s32[]{:S(2)}) async-start(), calls=%async_computation.3 | async-start | bytes 7864320 | tf_op jit(solution)/shard_map/reduce_scatter | solution.py:83
  8.1 5.6 copy-start.1
  8.1 5.7 copy-start
Sparse Core Ops, SparseCore 0:
  8.9 402.0 all-gather.2
  412.5 401.7 all-gather.4
  1252.0 66.5 reduce-scatter.1
where the time goes:
time: 1330 us
  waiting for transfers between devices  869 us (65%)
  matrix products  237 us (18%)
  local copies, waits for them, and re-layouts  118 us (9%)
  other arithmetic  88.1 us (7%)
    all_gather x1, waiting for transfers between devices, on_device(): value_piece = lax.all_gather(values, 'blk', axis=0, tiled=True)  403 us
    all_gather x1, waiting for transfers between devices, on_device(): key_piece = lax.all_gather(keys, 'blk', axis=0, tiled=True)  397 us
    dot_general x8, matrix products, attend(): jnp.einsum('hqk,khd->qhd', weights.astype(jnp.bfloat16), value_piece.resh...  109 us
    dot_general x8, matrix products, attend(): jnp.einsum('qhd,khd->hqk', query_heads, key_piece.reshape(row_count, head...  106 us
    dynamic_slice x32, local copies, waits for them, and re-layouts, on_device(): lax.scan(advance, initial, (key_split, value_split, offsets))  96.7 us
    reduce_sum x8, other arithmetic, attend(): totals = totals * rescale + jnp.sum(weights, axis=-1)  78.7 us
    reduce_scatter x1, waiting for transfers between devices, on_device(): lax.psum_scatter(jnp.dot(attended, out_weight, preferred_element_type=jnp...  66.8 us
  transfers between devices with their start and end apart: 3, of which 3 were waited for; matrix products, arithmetic and copies ran while one was open for 0% of the time, Pallas kernels for 0%

commit v1 on v0

v1 whole, which is shorter than its diff:
```python
import functools
import math

import jax
import jax.numpy as jnp
from jax import lax
from jax.experimental import pallas as pl
from jax.experimental.pallas import tpu as pltpu
from jax.sharding import PartitionSpec as P

HD = 128
BS = 128
KB = 16
GROUP = 4


class Plan:
    def __init__(self, heads, devices):
        self.heads, self.devices = heads, devices
        self.parts = 1
        while heads * self.parts % devices:
            self.parts *= 2
        self.each = heads * self.parts // devices
        self.slots = max(
            (self.each * b + self.each - 1) // self.parts - self.each * b // self.parts + 1
            for b in range(devices)
        )

    def first_head(self, handler):
        first = handler * self.each // self.parts
        if isinstance(first, int):
            return min(first, self.heads - self.slots)
        return jnp.minimum(first, self.heads - self.slots)

    def active(self, home, handler, slot):
        unit = (self.first_head(handler) + slot) * self.parts + home * self.parts // self.devices
        return (unit >= handler * self.each) & (unit < handler * self.each + self.each)

    def pairs(self, hop, slot):
        return [
            (home, home ^ hop)
            for home in range(self.devices)
            if self.active(home, home ^ hop, slot)
        ]


def pack(plan, slot, queries, keys, values):
    rows = queries.shape[0]
    count = plan.devices

    def body(q_ref, k_ref, v_ref, *rest):
        q_outs, kv_outs, sems = rest[:count], rest[count : 2 * count], rest[2 * count]
        me = lax.axis_index("blk")
        copies = []
        for hop in range(count):
            head = plan.first_head(me ^ hop) + slot
            columns = pl.ds(pl.multiple_of(head * HD, HD), HD)
            for n, (src, dst) in enumerate(
                ((k_ref, kv_outs[hop].at[0]), (v_ref, kv_outs[hop].at[1]), (q_ref, q_outs[hop]))
            ):
                copy = pltpu.make_async_copy(src.at[:, columns], dst, sems.at[hop, n])
                copy.start()
                copies.append(copy)
        for copy in copies:
            copy.wait()

    any_spec = pl.BlockSpec(memory_space=pl.ANY)
    outs = pl.pallas_call(
        body,
        out_shape=[jax.ShapeDtypeStruct((rows, HD), queries.dtype)] * count
        + [jax.ShapeDtypeStruct((2, rows, HD), queries.dtype)] * count,
        in_specs=[any_spec] * 3,
        out_specs=[any_spec] * (2 * count),
        scratch_shapes=[pltpu.SemaphoreType.DMA((count, 3))],
        cost_estimate=pl.CostEstimate(
            flops=0, bytes_accessed=12 * count * rows * HD, transcendentals=0
        ),
    )(queries, keys, values)
    return outs[:count], outs[count:]


def attend(plan, lists, counts, query_parts, kv_parts):
    count = plan.devices
    rows = query_parts[0].shape[0]
    blocks = rows // BS
    factor = math.log2(math.e) / math.sqrt(HD)

    def body(list_ref, count_ref, *rest):
        q_in, kv_in = rest[:count], rest[count : 2 * count]
        outs = rest[2 * count : 3 * count]
        q_ref, kv_ref, o_ref, s_ref, sems = rest[3 * count :]
        copies = []
        for hop in range(count):
            copies.append(pltpu.make_async_copy(kv_in[hop], kv_ref.at[hop], sems.at[0, hop]))
            copies.append(pltpu.make_async_copy(q_in[hop], q_ref.at[hop], sems.at[1, hop]))
        for copy in copies:
            copy.start()
        for copy in copies:
            copy.wait()

        def one(i, carry):
            used = count_ref[i]
            hop = i // blocks
            span = pl.ds(pl.multiple_of(lax.rem(i, blocks) * BS, BS), BS)

            @pl.when(used > 0)
            def _():
                query = q_ref[hop, span, :]
                groups = (used + GROUP - 1) // GROUP

                def score(g, highest):
                    for j in range(GROUP):
                        place = g * GROUP + j
                        at = list_ref[i * KB + place]
                        key = kv_ref[
                            at // blocks, 0, pl.ds(pl.multiple_of(lax.rem(at, blocks) * BS, BS), BS), :
                        ]
                        scores = lax.dot_general(
                            query, key, (((1,), (1,)), ((), ())), preferred_element_type=jnp.float32
                        )
                        scores = jnp.where(place < used, scores, -1e30)
                        s_ref[place] = scores
                        highest = jnp.maximum(highest, scores)
                    return highest

                highest = lax.fori_loop(
                    0, groups, score, jnp.full((BS, BS), -1e30, jnp.float32)
                )
                highest = jnp.max(highest, axis=1, keepdims=True)

                def weigh(g, state):
                    total, mixed = state
                    for j in range(GROUP):
                        place = g * GROUP + j
                        at = list_ref[i * KB + place]
                        value = kv_ref[
                            at // blocks, 1, pl.ds(pl.multiple_of(lax.rem(at, blocks) * BS, BS), BS), :
                        ]
                        weights = jnp.exp2((s_ref[place] - highest) * factor)
                        total = total + weights
                        mixed = mixed + jnp.dot(
                            weights.astype(jnp.bfloat16), value, preferred_element_type=jnp.float32
                        )
                    return total, mixed

                zero = jnp.zeros((BS, BS), jnp.float32)
                total, mixed = lax.fori_loop(0, groups, weigh, (zero, zero))
                total = jnp.sum(total, axis=1, keepdims=True)
                o_ref[hop, span, :] = (mixed / total).astype(jnp.bfloat16)

            return carry

        lax.fori_loop(0, count * blocks, one, 0)
        copies = [
            pltpu.make_async_copy(o_ref.at[hop], outs[hop], sems.at[0, hop])
            for hop in range(count)
        ]
        for copy in copies:
            copy.start()
        for copy in copies:
            copy.wait()

    any_spec = pl.BlockSpec(memory_space=pl.ANY)
    smem = pl.BlockSpec(memory_space=pltpu.SMEM)
    return pl.pallas_call(
        body,
        out_shape=[jax.ShapeDtypeStruct((rows, HD), jnp.bfloat16)] * count,
        in_specs=[smem, smem] + [any_spec] * (2 * count),
        out_specs=[any_spec] * count,
        scratch_shapes=[
            pltpu.VMEM((count, rows, HD), jnp.bfloat16),
            pltpu.VMEM((count, 2, rows, HD), jnp.bfloat16),
            pltpu.VMEM((count, rows, HD), jnp.bfloat16),
            pltpu.VMEM((KB, BS, BS), jnp.float32),
            pltpu.SemaphoreType.DMA((2, count)),
        ],
        compiler_params=pltpu.CompilerParams(vmem_limit_bytes=32 * 1024 * 1024),
        cost_estimate=pl.CostEstimate(
            flops=4 * count * rows * BS * HD * KB,
            bytes_accessed=8 * count * rows * HD,
            transcendentals=count * rows * BS * KB,
        ),
    )(lists, counts, *query_parts, *kv_parts)


def unpack(plan, returned):
    rows = returned[0][0].shape[0]
    count = plan.devices

    def body(*refs):
        parts, out_ref, sems = refs[:-2], refs[-2], refs[-1]
        me = lax.axis_index("blk")

        def each(act):
            for slot in range(plan.slots):
                for hop in range(count):
                    handler = me ^ hop
                    head = plan.first_head(handler) + slot
                    columns = pl.ds(pl.multiple_of(head * HD, HD), HD)

                    @pl.when(plan.active(me, handler, slot))
                    def _():
                        act(
                            pltpu.make_async_copy(
                                parts[slot * count + hop], out_ref.at[:, columns], sems.at[slot, hop]
                            )
                        )

        each(lambda copy: copy.start())
        each(lambda copy: copy.wait())

    any_spec = pl.BlockSpec(memory_space=pl.ANY)
    flat = [part for of_slot in returned for part in of_slot]
    return pl.pallas_call(
        body,
        out_shape=jax.ShapeDtypeStruct((rows, plan.heads * HD), jnp.bfloat16),
        in_specs=[any_spec] * len(flat),
        out_specs=any_spec,
        scratch_shapes=[pltpu.SemaphoreType.DMA((plan.slots, count))],
        cost_estimate=pl.CostEstimate(
            flops=0, bytes_accessed=4 * plan.heads * rows * HD, transcendentals=0
        ),
    )(*flat)


def project(attended, out_weight):
    groups = lax.axis_size("head")
    mine = lax.axis_index("head")
    rows = attended.shape[0] // groups
    width = out_weight.shape[1]
    cuts = 4
    piece = width // cuts

    def share(owner, cut):
        return jnp.dot(
            lax.dynamic_slice_in_dim(attended, owner * rows, rows, 0),
            out_weight[:, cut * piece : (cut + 1) * piece],
            preferred_element_type=jnp.float32,
        ).astype(jnp.bfloat16)

    arrived = [
        [
            lax.ppermute(share(mine ^ hop, cut), "head", [(g, g ^ hop) for g in range(groups)])
            for hop in range(1, groups)
        ]
        for cut in range(cuts)
    ]
    done = []
    for cut in range(cuts):
        total = share(mine, cut).astype(jnp.float32)
        for part in arrived[cut]:
            total = total + part.astype(jnp.float32)
        done.append(total.astype(jnp.bfloat16))
    return jnp.concatenate(done, axis=1)


def on_device(queries, keys, values, block_list, block_count, out_weight):
    rows, width = queries.shape
    devices = lax.axis_size("blk")
    me = lax.axis_index("blk")
    plan = Plan(width // HD, devices)
    blocks = rows // BS
    hops = jnp.arange(devices, dtype=jnp.int32)
    homes = me ^ hops
    lists = lax.all_gather(block_list, "blk", axis=0)[homes]
    counts = lax.all_gather(block_count, "blk", axis=0)[homes]
    lists = ((lists // blocks) ^ me) * blocks + lists % blocks
    lists = lists.reshape(-1)

    returned = []
    for slot in range(plan.slots):
        query_parts, kv_parts = pack(plan, slot, queries, keys, values)
        query_parts, kv_parts = list(query_parts), list(kv_parts)
        for hop in range(1, devices):
            kv_parts[hop] = lax.ppermute(
                kv_parts[hop], "blk", [(b, b ^ hop) for b in range(devices)]
            )
            query_parts[hop] = lax.ppermute(query_parts[hop], "blk", plan.pairs(hop, slot))
        handled = jnp.where(plan.active(homes, me, slot)[:, None], counts, 0).reshape(-1)
        results = list(attend(plan, lists, handled, query_parts, kv_parts))
        for hop in range(1, devices):
            results[hop] = lax.ppermute(
                results[hop], "blk", [(handler, home) for home, handler in plan.pairs(hop, slot)]
            )
        returned.append(results)
    return project(unpack(plan, returned), out_weight)


def solution(mesh):
    placed = (
        P(("dp", "blk"), "head"),
        P(("dp", "blk"), "head"),
        P(("dp", "blk"), "head"),
        P(("dp", "blk"), None),
        P(("dp", "blk")),
        P("head", None),
    )
    return jax.shard_map(
        on_device,
        mesh=mesh,
        in_specs=placed,
        out_specs=P(("dp", "blk", "head"), None),
        check_vma=False,
    )
```

time: 1330 us -> 874 us (0.66)
  waiting for transfers between devices: 869 us -> 73.9 us
  Pallas kernels: 0 us -> 480 us
  matrix products: 237 us -> 27.8 us
  starting transfers between devices: 0.08 us -> 181 us
  other arithmetic: 88.1 us -> 1.78 us
  local copies, waits for them, and re-layouts: 118 us -> 37.6 us
  blocking collectives: 0 us -> 68.6 us
    all_gather x2 -> x0, waiting for transfers between devices: 800 us -> none  [the longest x1 403 us: on_device(): value_piece = lax.all_gather(values, 'blk', axis=0, tiled=True)]
    pallas_call x0 -> x7, Pallas kernels: none -> 480 us  [the longest x3 290 us: pack(): pl.pallas_call(body, out_shape=[jax.ShapeDtypeStruct((rows, HD), queries....]
    dot_general x25 -> x8, matrix products: 237 us -> 27.8 us  [share(): jnp.dot(lax.dynamic_slice_in_dim(attended, owner * rows, rows, 0), out_we...]
    ppermute x0 -> x67, starting transfers between devices: none -> 181 us  [the longest x21 71.3 us: on_device(): lax.ppermute(results[hop], 'blk', [(handler, home) for home, handler in p...]
    dynamic_slice x32 -> x0, local copies, waits for them, and re-layouts: 96.7 us -> none  [on_device(): lax.scan(advance, initial, (key_split, value_split, offsets))]
    reduce_sum x9 -> x0, other arithmetic: 78.8 us -> none  [the longest x8 78.7 us: attend(): totals = totals * rescale + jnp.sum(weights, axis=-1)]
    ppermute x0 -> x67, waiting for transfers between devices: none -> 73.9 us  [the longest x4 27.9 us: project(): lax.ppermute(share(mine ^ hop, cut), 'head', [(g, g ^ hop) for g in range...]
    reduce_scatter x1 -> x0, waiting for transfers between devices: 66.8 us -> none  [on_device(): lax.psum_scatter(jnp.dot(attended, out_weight, preferred_element_type=jnp...]
  transfers between devices with their start and end apart: 3 -> 67, of which waited for: 3 -> 14; matrix products, arithmetic and copies ran while one was open for 0% -> 2% of each run, Pallas kernels for 0% -> 35%
where the time goes in v1:
time: 874 us; the launch traced here: 873 us
  Pallas kernels  480 us (55%)
  starting transfers between devices  181 us (21%)
  waiting for transfers between devices  73.9 us (8%)
  blocking collectives  68.6 us (8%)
  local copies, waits for them, and re-layouts  37.6 us (4%)
  matrix products  27.8 us (3%)
    pallas_call x3, Pallas kernels, pack(): pl.pallas_call(body, out_shape=[jax.ShapeDtypeStruct((rows, HD), queries....  290 us
    pallas_call x3, Pallas kernels, attend(): pl.pallas_call(body, out_shape=[jax.ShapeDtypeStruct((rows, HD), jnp.bflo...  109 us
    pallas_call x1, Pallas kernels, unpack(): pl.pallas_call(body, out_shape=jax.ShapeDtypeStruct((rows, plan.heads * H...  80.7 us
    ppermute x21, starting transfers between devices, on_device(): lax.ppermute(results[hop], 'blk', [(handler, home) for home, handler in p...  71.3 us
    all_gather x1, blocking collectives, on_device(): lists = lax.all_gather(block_list, 'blk', axis=0)[homes]  56.8 us
    ppermute x21, starting transfers between devices, on_device(): lax.ppermute(query_parts[hop], 'blk', plan.pairs(hop, slot))  53.2 us
    ppermute x21, starting transfers between devices, on_device(): lax.ppermute(kv_parts[hop], 'blk', [(b, b ^ hop) for b in range(devices)])  52.4 us
    unnamed x205, local copies, waits for them, and re-layouts  36.1 us
  transfers between devices with their start and end apart: 67, of which 14 were waited for; matrix products, arithmetic and copies ran while one was open for 2% of the time, Pallas kernels for 35%

profile of v1, /device:TPU:10, one launch (start us, length us, event | category | flops | bytes accessed | tf_op | source)
XLA Modules:
  0.0 872.5 jit_solution(13519764949660027333)
XLA Ops:
  0.0 96.6 %shard_map.68 = (bf16[512,128]{1,0:T(8,128)(2,1)}, bf16[512,128]{1,0:T(8,128)(2,1)}, bf16[512,128]{1,0:T(8,128)(2,1)}, bf16[512,128]{1,0:T(8,128)(2,1)}, bf16[51...) custom-call(bf16[512,2560]{1,0:T(8,128)(2,1)} %q_ref.5, ...), custom_call_target="tpu_custom_call" | custom-call | bytes 6291456 | tf_op jit(solution)/shard_map/pallas_call | solution.py:68
  101.0 4.8 collective-permute-start.44
  117.0 96.6 %shard_map.66 = (bf16[512,128]{1,0:T(8,128)(2,1)}, bf16[512,128]{1,0:T(8,128)(2,1)}, bf16[512,128]{1,0:T(8,128)(2,1)}, bf16[512,128]{1,0:T(8,128)(2,1)}, bf16[51...) custom-call(bf16[512,2560]{1,0:T(8,128)(2,1)} %q_ref.5, ...), custom_call_target="tpu_custom_call" | custom-call | bytes 6291456 | tf_op jit(solution)/shard_map/pallas_call | solution.py:68
  227.6 96.6 %shard_map.64 = (bf16[512,128]{1,0:T(8,128)(2,1)}, bf16[512,128]{1,0:T(8,128)(2,1)}, bf16[512,128]{1,0:T(8,128)(2,1)}, bf16[512,128]{1,0:T(8,128)(2,1)}, bf16[51...) custom-call(bf16[512,2560]{1,0:T(8,128)(2,1)} %q_ref.5, ...), custom_call_target="tpu_custom_call" | custom-call | bytes 6291456 | tf_op jit(solution)/shard_map/pallas_call | solution.py:68
  331.5 5.6 collective-permute-start.2
  340.4 7.7 collective-permute-start.4
  358.3 5.0 collective-permute-start.51
  364.4 4.8 collective-permute-done.6.rest_7_
  373.6 18.3 %collective-permute-done.52.rest_12_ = bf16[2,512,128]{2,1,0:T(8,128)(2,1)S(1)} collective-permute-done((bf16[2,512,128]{2,1,0:T(8,128)(2,1)S(1)}, bf16[2,512,128]{2,1,0:T(8,128)(2,1)S(1)}, u32[]{:S(2)}, u32[]{:S(2)}) %collective-permute-start.52) | collective-permute-done | bytes 262176 | tf_op jit(solution)/shard_map/ppermute | solution.py:275
  392.0 4.2 collective-permute-start.29
  397.6 5.1 collective-permute-start.30
  407.4 11.8 %all-reduce = s32[32]{0:T(128)S(1)} all-reduce(s32[32]{0:T(128)S(1)} %dynamic-update-slice), channel_id=3, replica_groups=mesh['dp'=2,'blk'=8,'head'=2] {'blk'}, use_global_device_ids=true, to_apply=%add | all-reduce | flops 32 | bytes 256
  419.8 7.2 collective-permute-start.32
  427.1 5.7 collective-permute-start.33
  432.8 5.7 collective-permute-start.34
  441.6 56.8 %all-gather.2 = s32[8,4,16]{2,1,0:T(4,128)S(1)} all-gather(s32[1,4,16]{2,1,0:T(4,128)S(1)} %bitcast.4), channel_id=2, replica_groups=mesh['dp'=2,'blk'=8,'head'=2] {'blk'}, dimensions={0}, use_global_device_ids=true | all-gather | bytes 2304 | tf_op jit(solution)/shard_map/all_gather | solution.py:265
  501.3 5.7 collective-permute-start.13
  520.0 43.9 %shard_map.69 = (bf16[512,128]{1,0:T(8,128)(2,1)S(1)}, bf16[512,128]{1,0:T(8,128)(2,1)}, bf16[512,128]{1,0:T(8,128)(2,1)S(1)}, bf16[512,128]{1,0:T(8,128)(2,1)S(...) custom-call(s32[512]{0:T(512)S(1)} %fusion.86.list_ref, ...), custom_call_target="tpu_custom_call" | custom-call | flops 4294967296 | bytes 4194304 | tf_op jit(solution)/shard_map/pallas_call | solution.py:165
  580.6 4.8 collective-permute-start.60
  593.8 44.7 %shard_map.67 = (bf16[512,128]{1,0:T(8,128)(2,1)S(1)}, bf16[512,128]{1,0:T(8,128)(2,1)S(1)}, bf16[512,128]{1,0:T(8,128)(2,1)S(1)}, bf16[512,128]{1,0:T(8,128)(2,...) custom-call(s32[512]{0:T(512)S(1)} %fusion.86.list_ref, ...), custom_call_target="tpu_custom_call" | custom-call | flops 4294967296 | bytes 4194304 | tf_op jit(solution)/shard_map/pallas_call | solution.py:165
  648.2 20.9 %shard_map.65 = (bf16[512,128]{1,0:T(8,128)(2,1)S(1)}, bf16[512,128]{1,0:T(8,128)(2,1)S(1)}, bf16[512,128]{1,0:T(8,128)(2,1)S(1)}, bf16[512,128]{1,0:T(8,128)(2,...) custom-call(s32[512]{0:T(512)S(1)} %fusion.86.list_ref, ...), custom_call_target="tpu_custom_call" | custom-call | flops 4294967296 | bytes 4194304 | tf_op jit(solution)/shard_map/pallas_call | solution.py:165
  669.7 25.3 %collective-permute-start.39 = (bf16[512,128]{1,0:T(8,128)(2,1)S(1)}, bf16[512,128]{1,0:T(8,128)(2,1)S(1)}, u32[]{:S(2)}, u32[]{:S(2)}) collective-permute-start(bf16[512,128]{1,0:T(8,128)(2,1)S(1)} %get-tuple-element.122), channel_id=1, source_target_pairs={{10,0},{8,2},{14,4},{12,6},{2,8},{0,10},{6,12},{4,14},{11,1},{9,3}... | collective-permute-start | bytes 393224 | tf_op jit(solution)/shard_map/ppermute | solution.py:282
  700.4 7.9 collective-permute-done.40.refs_14_
  724.2 5.6 collective-permute-done.20.refs_7_
  730.4 80.7 %shard_map.70 = bf16[512,2560]{1,0:T(8,128)(2,1)} custom-call(bf16[512,128]{1,0:T(8,128)(2,1)} %copy-done.2, bf16[512,128]{1,0:T(8,128)(2,1)} %copy-done.77, bf16[512,128]{1,0:T(8,128)(2,1)} %copy-done.78, bf16[512,128]{1,0:T(8,128)(2,1)} %copy-done.79, bf16[512,128]{1,0:T(8,128)(2,1)} %copy-done.80, bf16[512,128]{1,0:T(8,128)(2,1)} %copy-done.81, ...), custom_call_target="tpu_custom_call" | custom-call | bytes 5242880 | tf_op jit(solution)/shard_map/pallas_call | solution.py:214
  811.2 5.3 fusion.25
  816.5 4.9 fusion.37
  822.9 5.4 fusion.49
  828.5 4.8 fusion.61
  841.0 12.1 %collective-permute-done.64 = bf16[256,1280]{1,0:T(8,128)(2,1)S(1)} collective-permute-done((bf16[256,1280]{1,0:T(8,128)(2,1)S(1)}, bf16[256,1280]{1,0:T(8,128)(2,1)S(1)}, u32[]{:S(2)}, u32[]{:S(2)}) %collective-permute-start.64) | collective-permute-done | bytes 655392 | tf_op jit(solution)/shard_map/ppermute | solution.py:243
  855.0 6.9 collective-permute-done.65
  863.8 5.2 collective-permute-done.66
  (339 shorter events, 153.8 us)
Async XLA Ops:
  101.0 112.7 %collective-permute-start.44 = (bf16[512,128]{1,0:T(8,128)(2,1)}, bf16[512,128]{1,0:T(8,128)(2,1)S(1)}, u32[]{:S(2)}, u32[]{:S(2)}) collective-permute-start(bf16[512,128]{1,0:T(8,128)(2,1)} %get-tuple-element.128), channel_id=1, source_target_pairs={{0,6},{2,4},{4,2},{6,0},{8,14},{12,10},{1,7},{3,5},{5,3},{7,1},{9,... | collective-permute-start | bytes 393224 | tf_op jit(solution)/shard_map/ppermute | solution.py:278
  105.8 110.6 %collective-permute-start.45 = (bf16[512,128]{1,0:T(8,128)(2,1)}, bf16[512,128]{1,0:T(8,128)(2,1)S(1)}, u32[]{:S(2)}, u32[]{:S(2)}) collective-permute-start(bf16[512,128]{1,0:T(8,128)(2,1)} %get-tuple-element.129), channel_id=1, source_target_pairs={{0,8},{2,10},{4,12},{6,14},{10,2},{14,6},{1,9},{3,11},{5,13},{7,15... | collective-permute-start | bytes 393224 | tf_op jit(solution)/shard_map/ppermute | solution.py:278
  107.8 111.6 %collective-permute-start.46 = (bf16[512,128]{1,0:T(8,128)(2,1)}, bf16[512,128]{1,0:T(8,128)(2,1)S(1)}, u32[]{:S(2)}, u32[]{:S(2)}) collective-permute-start(bf16[512,128]{1,0:T(8,128)(2,1)} %get-tuple-element.130), channel_id=1, source_target_pairs={{0,10},{2,8},{4,14},{6,12},{8,2},{12,6},{1,11},{3,9},{5,15},{7,13}... | collective-permute-start | bytes 393224 | tf_op jit(solution)/shard_map/ppermute | solution.py:278
  111.1 108.9 %collective-permute-start.47 = (bf16[512,128]{1,0:T(8,128)(2,1)}, bf16[512,128]{1,0:T(8,128)(2,1)S(1)}, u32[]{:S(2)}, u32[]{:S(2)}) collective-permute-start(bf16[512,128]{1,0:T(8,128)(2,1)} %get-tuple-element.131), channel_id=1, source_target_pairs={{0,12},{2,14},{4,8},{6,10},{10,6},{14,2},{1,13},{3,15},{5,9},{7,11... | collective-permute-start | bytes 393224 | tf_op jit(solution)/shard_map/ppermute | solution.py:278
  114.2 109.0 %collective-permute-start.48 = (bf16[512,128]{1,0:T(8,128)(2,1)}, bf16[512,128]{1,0:T(8,128)(2,1)S(1)}, u32[]{:S(2)}, u32[]{:S(2)}) collective-permute-start(bf16[512,128]{1,0:T(8,128)(2,1)} %get-tuple-element.132), channel_id=1, source_target_pairs={{0,14},{2,12},{4,10},{6,8},{8,6},{12,2},{1,15},{3,13},{5,11},{7,9}... | collective-permute-start | bytes 393224 | tf_op jit(solution)/shard_map/ppermute | solution.py:278
  217.1 107.1 %collective-permute-start.22 = (bf16[512,128]{1,0:T(8,128)(2,1)}, bf16[512,128]{1,0:T(8,128)(2,1)S(1)}, u32[]{:S(2)}, u32[]{:S(2)}) collective-permute-start(bf16[512,128]{1,0:T(8,128)(2,1)} %get-tuple-element.103), channel_id=1, source_target_pairs={{0,4},{2,6},{4,0},{6,2},{8,12},{10,14},{12,8},{14,10},{1,5},{3,7},... | collective-permute-start | bytes 393224 | tf_op jit(solution)/shard_map/ppermute | solution.py:278
  220.0 105.4 %collective-permute-start.23 = (bf16[512,128]{1,0:T(8,128)(2,1)}, bf16[512,128]{1,0:T(8,128)(2,1)S(1)}, u32[]{:S(2)}, u32[]{:S(2)}) collective-permute-start(bf16[512,128]{1,0:T(8,128)(2,1)} %get-tuple-element.104), channel_id=1, source_target_pairs={{0,6},{2,4},{4,2},{6,0},{8,14},{10,12},{12,10},{14,8},{1,7},{3,5},... | collective-permute-start | bytes 393224 | tf_op jit(solution)/shard_map/ppermute | solution.py:278
  220.7 108.8 %collective-permute-start.24 = (bf16[512,128]{1,0:T(8,128)(2,1)}, bf16[512,128]{1,0:T(8,128)(2,1)S(1)}, u32[]{:S(2)}, u32[]{:S(2)}) collective-permute-start(bf16[512,128]{1,0:T(8,128)(2,1)} %get-tuple-element.105), channel_id=1, source_target_pairs={{0,8},{2,10},{4,12},{6,14},{8,0},{10,2},{12,4},{14,6},{1,9},{3,11}... | collective-permute-start | bytes 393224 | tf_op jit(solution)/shard_map/ppermute | solution.py:278
  223.9 107.0 %collective-permute-start.25 = (bf16[512,128]{1,0:T(8,128)(2,1)}, bf16[512,128]{1,0:T(8,128)(2,1)S(1)}, u32[]{:S(2)}, u32[]{:S(2)}) collective-permute-start(bf16[512,128]{1,0:T(8,128)(2,1)} %get-tuple-element.106), channel_id=1, source_target_pairs={{0,10},{2,8},{4,14},{6,12},{8,2},{10,0},{12,6},{14,4},{1,11},{3,9}... | collective-permute-start | bytes 393224 | tf_op jit(solution)/shard_map/ppermute | solution.py:278
  226.1 111.1 %collective-permute-start.26 = (bf16[512,128]{1,0:T(8,128)(2,1)}, bf16[512,128]{1,0:T(8,128)(2,1)S(1)}, u32[]{:S(2)}, u32[]{:S(2)}) collective-permute-start(bf16[512,128]{1,0:T(8,128)(2,1)} %get-tuple-element.107), channel_id=1, source_target_pairs={{0,12},{2,14},{4,8},{6,10},{8,4},{10,6},{12,0},{14,2},{1,13},{3,15... | collective-permute-start | bytes 393224 | tf_op jit(solution)/shard_map/ppermute | solution.py:278
  370.1 49.7 %collective-permute-start.55 = (bf16[2,512,128]{2,1,0:T(8,128)(2,1)S(1)}, bf16[2,512,128]{2,1,0:T(8,128)(2,1)S(1)}, u32[]{:S(2)}, u32[]{:S(2)}) collective-permute-start(bf16[2,512,128]{2,1,0:T(8,128)(2,1)S(1)} %copy-done.85), channel_id=1, source_target_pairs={{0,14},{2,12},{4,10},{6,8},{8,6},{10,4},{12,2},{14,0},{1,15},{3,13... | collective-permute-start | bytes 786440 | tf_op jit(solution)/shard_map/ppermute | solution.py:275
  373.3 53.7 %collective-permute-start.28 = (bf16[2,512,128]{2,1,0:T(8,128)(2,1)}, bf16[2,512,128]{2,1,0:T(8,128)(2,1)S(1)}, u32[]{:S(2)}, u32[]{:S(2)}) collective-permute-start(bf16[2,512,128]{2,1,0:T(8,128)(2,1)} %get-tuple-element.110), channel_id=1, source_target_pairs={{0,2},{2,0},{4,6},{6,4},{8,10},{10,8},{12,14},{14,12},{1,3},{3,1},... | collective-permute-start | bytes 786440 | tf_op jit(solution)/shard_map/ppermute | solution.py:275
  397.6 40.9 %collective-permute-start.30 = (bf16[2,512,128]{2,1,0:T(8,128)(2,1)}, bf16[2,512,128]{2,1,0:T(8,128)(2,1)S(1)}, u32[]{:S(2)}, u32[]{:S(2)}) collective-permute-start(bf16[2,512,128]{2,1,0:T(8,128)(2,1)} %get-tuple-element.112), channel_id=1, source_target_pairs={{0,6},{2,4},{4,2},{6,0},{8,14},{10,12},{12,10},{14,8},{1,7},{3,5},... | collective-permute-start | bytes 786440 | tf_op jit(solution)/shard_map/ppermute | solution.py:275
  419.8 79.3 %collective-permute-start.32 = (bf16[2,512,128]{2,1,0:T(8,128)(2,1)}, bf16[2,512,128]{2,1,0:T(8,128)(2,1)}, u32[]{:S(2)}, u32[]{:S(2)}) collective-permute-start(bf16[2,512,128]{2,1,0:T(8,128)(2,1)} %get-tuple-element.114), channel_id=1, source_target_pairs={{0,10},{2,8},{4,14},{6,12},{8,2},{10,0},{12,6},{14,4},{1,11},{3,9}... | collective-permute-start | bytes 786440 | tf_op jit(solution)/shard_map/ppermute | solution.py:275
  427.1 74.2 %collective-permute-start.33 = (bf16[2,512,128]{2,1,0:T(8,128)(2,1)}, bf16[2,512,128]{2,1,0:T(8,128)(2,1)}, u32[]{:S(2)}, u32[]{:S(2)}) collective-permute-start(bf16[2,512,128]{2,1,0:T(8,128)(2,1)} %get-tuple-element.115), channel_id=1, source_target_pairs={{0,12},{2,14},{4,8},{6,10},{8,4},{10,6},{12,0},{14,2},{1,13},{3,15... | collective-permute-start | bytes 786440 | tf_op jit(solution)/shard_map/ppermute | solution.py:275
  432.8 74.1 %collective-permute-start.34 = (bf16[2,512,128]{2,1,0:T(8,128)(2,1)}, bf16[2,512,128]{2,1,0:T(8,128)(2,1)}, u32[]{:S(2)}, u32[]{:S(2)}) collective-permute-start(bf16[2,512,128]{2,1,0:T(8,128)(2,1)} %get-tuple-element.116), channel_id=1, source_target_pairs={{0,14},{2,12},{4,10},{6,8},{8,6},{10,4},{12,2},{14,0},{1,15},{3,13... | collective-permute-start | bytes 786440 | tf_op jit(solution)/shard_map/ppermute | solution.py:275
  438.5 68.4 %collective-permute-start.10 = (bf16[2,512,128]{2,1,0:T(8,128)(2,1)}, bf16[2,512,128]{2,1,0:T(8,128)(2,1)S(1)}, u32[]{:S(2)}, u32[]{:S(2)}) collective-permute-start(bf16[2,512,128]{2,1,0:T(8,128)(2,1)} %get-tuple-element.89), channel_id=1, source_target_pairs={{0,8},{2,10},{4,12},{6,14},{8,0},{10,2},{12,4},{14,6},{1,9},{3,11}... | collective-permute-start | bytes 786440 | tf_op jit(solution)/shard_map/ppermute | solution.py:275
  441.0 70.3 %collective-permute-start.11 = (bf16[2,512,128]{2,1,0:T(8,128)(2,1)}, bf16[2,512,128]{2,1,0:T(8,128)(2,1)}, u32[]{:S(2)}, u32[]{:S(2)}) collective-permute-start(bf16[2,512,128]{2,1,0:T(8,128)(2,1)} %get-tuple-element.90), channel_id=1, source_target_pairs={{0,10},{2,8},{4,14},{6,12},{8,2},{10,0},{12,6},{14,4},{1,11},{3,9}... | collective-permute-start | bytes 786440 | tf_op jit(solution)/shard_map/ppermute | solution.py:275
  499.1 69.3 %collective-permute-start.12 = (bf16[2,512,128]{2,1,0:T(8,128)(2,1)}, bf16[2,512,128]{2,1,0:T(8,128)(2,1)S(1)}, u32[]{:S(2)}, u32[]{:S(2)}) collective-permute-start(bf16[2,512,128]{2,1,0:T(8,128)(2,1)} %get-tuple-element.91), channel_id=1, source_target_pairs={{0,12},{2,14},{4,8},{6,10},{8,4},{10,6},{12,0},{14,2},{1,13},{3,15... | collective-permute-start | bytes 786440 | tf_op jit(solution)/shard_map/ppermute | solution.py:275
  501.3 70.0 %collective-permute-start.13 = (bf16[2,512,128]{2,1,0:T(8,128)(2,1)}, bf16[2,512,128]{2,1,0:T(8,128)(2,1)}, u32[]{:S(2)}, u32[]{:S(2)}) collective-permute-start(bf16[2,512,128]{2,1,0:T(8,128)(2,1)} %get-tuple-element.92), channel_id=1, source_target_pairs={{0,14},{2,12},{4,10},{6,8},{8,6},{10,4},{12,2},{14,0},{1,15},{3,13... | collective-permute-start | bytes 786440 | tf_op jit(solution)/shard_map/ppermute | solution.py:275
  507.0 68.3 %collective-permute-start.7 = (bf16[2,512,128]{2,1,0:T(8,128)(2,1)}, bf16[2,512,128]{2,1,0:T(8,128)(2,1)}, u32[]{:S(2)}, u32[]{:S(2)}) collective-permute-start(bf16[2,512,128]{2,1,0:T(8,128)(2,1)} %get-tuple-element.86), channel_id=1, source_target_pairs={{0,2},{2,0},{4,6},{6,4},{8,10},{10,8},{12,14},{14,12},{1,3},{3,1},... | collective-permute-start | bytes 786440 | tf_op jit(solution)/shard_map/ppermute | solution.py:275
  507.7 70.9 %collective-permute-start.8 = (bf16[2,512,128]{2,1,0:T(8,128)(2,1)}, bf16[2,512,128]{2,1,0:T(8,128)(2,1)}, u32[]{:S(2)}, u32[]{:S(2)}) collective-permute-start(bf16[2,512,128]{2,1,0:T(8,128)(2,1)} %get-tuple-element.87), channel_id=1, source_target_pairs={{0,4},{2,6},{4,0},{6,2},{8,12},{10,14},{12,8},{14,10},{1,5},{3,7},... | collective-permute-start | bytes 786440 | tf_op jit(solution)/shard_map/ppermute | solution.py:275
  511.3 69.2 %collective-permute-start.9 = (bf16[2,512,128]{2,1,0:T(8,128)(2,1)}, bf16[2,512,128]{2,1,0:T(8,128)(2,1)}, u32[]{:S(2)}, u32[]{:S(2)}) collective-permute-start(bf16[2,512,128]{2,1,0:T(8,128)(2,1)} %get-tuple-element.88), channel_id=1, source_target_pairs={{0,6},{2,4},{4,2},{6,0},{8,14},{10,12},{12,10},{14,8},{1,7},{3,5},... | collective-permute-start | bytes 786440 | tf_op jit(solution)/shard_map/ppermute | solution.py:275
  571.3 67.9 %collective-permute-start.57 = (bf16[512,128]{1,0:T(8,128)(2,1)}, bf16[512,128]{1,0:T(8,128)(2,1)S(1)}, u32[]{:S(2)}, u32[]{:S(2)}) collective-permute-start(bf16[512,128]{1,0:T(8,128)(2,1)} %copy-done.61), channel_id=1, source_target_pairs={{4,0},{6,2},{0,4},{2,6},{14,10},{10,14},{5,1},{7,3},{1,5},{3,7},{1... | collective-permute-start | bytes 393224 | tf_op jit(solution)/shard_map/ppermute | solution.py:282
  575.2 66.7 %collective-permute-start.58 = (bf16[512,128]{1,0:T(8,128)(2,1)}, bf16[512,128]{1,0:T(8,128)(2,1)S(1)}, u32[]{:S(2)}, u32[]{:S(2)}) collective-permute-start(bf16[512,128]{1,0:T(8,128)(2,1)} %copy-done.60), channel_id=1, source_target_pairs={{6,0},{4,2},{2,4},{0,6},{14,8},{10,12},{7,1},{5,3},{3,5},{1,7},{15... | collective-permute-start | bytes 393224 | tf_op jit(solution)/shard_map/ppermute | solution.py:282
  578.6 63.4 %collective-permute-start.59 = (bf16[512,128]{1,0:T(8,128)(2,1)}, bf16[512,128]{1,0:T(8,128)(2,1)S(1)}, u32[]{:S(2)}, u32[]{:S(2)}) collective-permute-start(bf16[512,128]{1,0:T(8,128)(2,1)} %copy-done.59), channel_id=1, source_target_pairs={{8,0},{10,2},{12,4},{14,6},{2,10},{6,14},{9,1},{11,3},{13,5},{15,7... | collective-permute-start | bytes 393224 | tf_op jit(solution)/shard_map/ppermute | solution.py:282
  580.6 62.5 %collective-permute-start.60 = (bf16[512,128]{1,0:T(8,128)(2,1)}, bf16[512,128]{1,0:T(8,128)(2,1)S(1)}, u32[]{:S(2)}, u32[]{:S(2)}) collective-permute-start(bf16[512,128]{1,0:T(8,128)(2,1)} %copy-done.58), channel_id=1, source_target_pairs={{10,0},{8,2},{14,4},{12,6},{2,8},{6,12},{11,1},{9,3},{15,5},{13,7}... | collective-permute-start | bytes 393224 | tf_op jit(solution)/shard_map/ppermute | solution.py:282
  585.4 60.1 %collective-permute-start.61 = (bf16[512,128]{1,0:T(8,128)(2,1)}, bf16[512,128]{1,0:T(8,128)(2,1)S(1)}, u32[]{:S(2)}, u32[]{:S(2)}) collective-permute-start(bf16[512,128]{1,0:T(8,128)(2,1)} %copy-done.57), channel_id=1, source_target_pairs={{12,0},{14,2},{8,4},{10,6},{6,10},{2,14},{13,1},{15,3},{9,5},{11,7... | collective-permute-start | bytes 393224 | tf_op jit(solution)/shard_map/ppermute | solution.py:282
  642.0 53.0 %collective-permute-start.35 = (bf16[512,128]{1,0:T(8,128)(2,1)S(1)}, bf16[512,128]{1,0:T(8,128)(2,1)S(1)}, u32[]{:S(2)}, u32[]{:S(2)}) collective-permute-start(bf16[512,128]{1,0:T(8,128)(2,1)S(1)} %get-tuple-element.118), channel_id=1, source_target_pairs={{2,0},{0,2},{6,4},{4,6},{10,8},{8,10},{14,12},{12,14},{3,1},{1,3},... | collective-permute-start | bytes 393224 | tf_op jit(solution)/shard_map/ppermute | solution.py:282
  642.1 54.4 %collective-permute-start.36 = (bf16[512,128]{1,0:T(8,128)(2,1)S(1)}, bf16[512,128]{1,0:T(8,128)(2,1)S(1)}, u32[]{:S(2)}, u32[]{:S(2)}) collective-permute-start(bf16[512,128]{1,0:T(8,128)(2,1)S(1)} %get-tuple-element.119), channel_id=1, source_target_pairs={{4,0},{6,2},{0,4},{2,6},{12,8},{14,10},{8,12},{10,14},{5,1},{7,3},... | collective-permute-start | bytes 393224 | tf_op jit(solution)/shard_map/ppermute | solution.py:282
  643.1 54.0 %collective-permute-start.37 = (bf16[512,128]{1,0:T(8,128)(2,1)S(1)}, bf16[512,128]{1,0:T(8,128)(2,1)S(1)}, u32[]{:S(2)}, u32[]{:S(2)}) collective-permute-start(bf16[512,128]{1,0:T(8,128)(2,1)S(1)} %get-tuple-element.120), channel_id=1, source_target_pairs={{6,0},{4,2},{2,4},{0,6},{14,8},{12,10},{10,12},{8,14},{7,1},{5,3},... | collective-permute-start | bytes 393224 | tf_op jit(solution)/shard_map/ppermute | solution.py:282
  645.6 52.8 %collective-permute-start.38 = (bf16[512,128]{1,0:T(8,128)(2,1)S(1)}, bf16[512,128]{1,0:T(8,128)(2,1)S(1)}, u32[]{:S(2)}, u32[]{:S(2)}) collective-permute-start(bf16[512,128]{1,0:T(8,128)(2,1)S(1)} %get-tuple-element.121), channel_id=1, source_target_pairs={{8,0},{10,2},{12,4},{14,6},{0,8},{2,10},{4,12},{6,14},{9,1},{11,3}... | collective-permute-start | bytes 393224 | tf_op jit(solution)/shard_map/ppermute | solution.py:282
  (136 other events, 3883.1 us)

commit v2 on v1

v2 whole, which is shorter than its diff:
```python
import functools
import math

import jax
import jax.numpy as jnp
from jax import lax
from jax.experimental import pallas as pl
from jax.experimental.pallas import tpu as pltpu
from jax.sharding import PartitionSpec as P

HD = 128
BS = 128
KB = 16
GROUP = 8
META = 8
MESH = pl.DeviceIdType.MESH


class Plan:
    def __init__(self, heads, devices):
        self.heads, self.devices = heads, devices
        self.parts = 1
        while heads * self.parts % devices:
            self.parts *= 2
        self.each = heads * self.parts // devices
        firsts = [self.each * b // self.parts for b in range(devices)]
        lasts = [(self.each * b + self.each - 1) // self.parts for b in range(devices)]
        self.slots = max(last - first + 1 for first, last in zip(firsts, lasts))
        self.clipped = max(firsts) > heads - self.slots

    def first_head(self, handler):
        first = handler * self.each // self.parts
        if self.clipped:
            first = jnp.minimum(first, self.heads - self.slots)
        return first

    def handler(self, home, head):
        return (head * self.parts + home * self.parts // self.devices) // self.each

    def active(self, home, handler, slot):
        return self.handler(home, self.first_head(handler) + slot) == handler


def greet(count):
    me = lax.axis_index("blk")
    barrier = pltpu.get_barrier_semaphore()
    for hop in range(1, count):
        pl.semaphore_signal(
            barrier, inc=1, device_id={"blk": (me + hop) % count}, device_id_type=MESH
        )
    pl.semaphore_wait(barrier, count - 1)


def exchange(plan, queries, keys, values, table):
    rows = queries.shape[0]
    count, slots = plan.devices, plan.slots

    def body(q_ref, k_ref, v_ref, t_ref, out, t_out, held, sends, recvs, t_sends, t_recvs, own):
        me = lax.axis_index("blk")

        def big(slot, hop, both):
            part = pl.ds(0, 2) if both else pl.ds(2, 1)
            which = 0 if both else 1
            return pltpu.make_async_remote_copy(
                src_ref=held.at[slot, hop, part],
                dst_ref=out.at[slot, hop, part],
                send_sem=sends.at[slot, hop, which],
                recv_sem=recvs.at[slot, hop, which],
                device_id={"blk": (me + hop) % count},
                device_id_type=MESH,
            )

        def small(hop):
            return pltpu.make_async_remote_copy(
                src_ref=t_ref,
                dst_ref=t_out.at[hop],
                send_sem=t_sends.at[hop],
                recv_sem=t_recvs.at[hop],
                device_id={"blk": (me + hop) % count},
                device_id_type=MESH,
            )

        greet(count)
        own_table = pltpu.make_async_copy(t_ref, t_out.at[0], own.at[slots])
        own_table.start()
        for hop in range(1, count):
            small(hop).start()
        order = sorted(range(1, count), key=lambda hop: -min(hop, count - hop))
        for slot in range(slots):
            for hop in order + [0]:
                handler = (me + hop) % count
                head = plan.first_head(handler) + slot
                columns = pl.ds(pl.multiple_of(head * HD, HD), HD)
                held[slot, hop, 0] = k_ref[:, columns]
                held[slot, hop, 1] = v_ref[:, columns]
                held[slot, hop, 2] = q_ref[:, columns]
                if hop == 0:
                    pltpu.make_async_copy(held.at[slot, 0], out.at[slot, 0], own.at[slot]).start()
                    continue
                big(slot, hop, True).start()

                @pl.when(plan.active(me, handler, slot))
                def _():
                    big(slot, hop, False).start()

        for slot in range(slots):
            for hop in range(1, count):
                big(slot, hop, True).wait()

                @pl.when(plan.active(me, (me + hop) % count, slot))
                def _():
                    big(slot, hop, False).wait_send()

                @pl.when(plan.active((me + count - hop) % count, me, slot))
                def _():
                    big(slot, hop, False).wait_recv()

            pltpu.make_async_copy(held.at[slot, 0], out.at[slot, 0], own.at[slot]).wait()
        for hop in range(1, count):
            small(hop).wait()
        own_table.wait()

    any_spec = pl.BlockSpec(memory_space=pl.ANY)
    vmem = pl.BlockSpec(memory_space=pltpu.VMEM)
    dma = pltpu.SemaphoreType.DMA
    return pl.pallas_call(
        body,
        out_shape=[
            jax.ShapeDtypeStruct((slots, count, 3, rows, HD), queries.dtype),
            jax.ShapeDtypeStruct((count, META, HD), jnp.int32),
        ],
        in_specs=[vmem] * 4,
        out_specs=[any_spec] * 2,
        scratch_shapes=[
            pltpu.VMEM((slots, count, 3, rows, HD), queries.dtype),
            dma((slots, count, 2)),
            dma((slots, count, 2)),
            dma((count,)),
            dma((count,)),
            dma((slots + 1,)),
        ],
        compiler_params=pltpu.CompilerParams(
            collective_id=0, has_side_effects=True, vmem_limit_bytes=48 * 1024 * 1024
        ),
        cost_estimate=pl.CostEstimate(
            flops=0, bytes_accessed=12 * slots * count * rows * HD, transcendentals=0
        ),
    )(queries, keys, values, table)


def attend(plan, lists, counts, packed):
    slots, count, _, rows, _ = packed.shape
    blocks = rows // BS
    factor = math.log2(math.e) / math.sqrt(HD)

    def body(list_ref, count_ref, in_ref, o_ref, s_ref):
        slot = pl.program_id(0)

        def listed(i, g, j, kind):
            at = list_ref[i * KB + g * GROUP + j]
            span = pl.ds(pl.multiple_of(lax.rem(at, blocks) * BS, BS), BS)
            return in_ref[0, at // blocks, kind, span, :]

        def one(i, carry):
            used = count_ref[slot * count * blocks + i]
            hop = i // blocks
            span = pl.ds(pl.multiple_of(lax.rem(i, blocks) * BS, BS), BS)

            @pl.when(used > 0)
            def _():
                query = in_ref[0, hop, 2, span, :]
                groups = (used + GROUP - 1) // GROUP

                def score(g, highest):
                    for j in range(0, GROUP, 2):
                        key = jnp.concatenate([listed(i, g, j, 0), listed(i, g, j + 1, 0)], axis=0)
                        pair = lax.dot_general(
                            query, key, (((1,), (1,)), ((), ())), preferred_element_type=jnp.float32
                        )
                        for n in range(2):
                            place = g * GROUP + j + n
                            scores = pair[:, n * BS : (n + 1) * BS]
                            scores = jnp.where(place < used, scores, -1e30)
                            s_ref[place] = scores
                            highest = jnp.maximum(highest, scores)
                    return highest

                highest = lax.fori_loop(
                    0, groups, score, jnp.full((BS, BS), -1e30, jnp.float32)
                )
                highest = jnp.max(highest, axis=1, keepdims=True)

                def weigh(g, state):
                    total, mixed = state
                    for j in range(0, GROUP, 2):
                        value = jnp.concatenate(
                            [listed(i, g, j, 1), listed(i, g, j + 1, 1)], axis=0
                        )
                        pair = []
                        for n in range(2):
                            weights = jnp.exp2((s_ref[g * GROUP + j + n] - highest) * factor)
                            total = total + weights
                            pair.append(weights.astype(jnp.bfloat16))
                        mixed = mixed + jnp.dot(
                            jnp.concatenate(pair, axis=1), value, preferred_element_type=jnp.float32
                        )
                    return total, mixed

                zero = jnp.zeros((BS, BS), jnp.float32)
                total, mixed = lax.fori_loop(0, groups, weigh, (zero, zero))
                total = jnp.sum(total, axis=1, keepdims=True)
                o_ref[0, hop, span, :] = (mixed / total).astype(jnp.bfloat16)

            return carry

        lax.fori_loop(0, count * blocks, one, 0)

    smem = pl.BlockSpec(memory_space=pltpu.SMEM)
    return pl.pallas_call(
        body,
        grid=(slots,),
        out_shape=jax.ShapeDtypeStruct((slots, count, rows, HD), jnp.bfloat16),
        in_specs=[
            smem,
            smem,
            pl.BlockSpec((1, count, 3, rows, HD), lambda slot: (slot, 0, 0, 0, 0)),
        ],
        out_specs=pl.BlockSpec((1, count, rows, HD), lambda slot: (slot, 0, 0, 0)),
        scratch_shapes=[pltpu.VMEM((KB, BS, BS), jnp.float32)],
        compiler_params=pltpu.CompilerParams(vmem_limit_bytes=48 * 1024 * 1024),
        cost_estimate=pl.CostEstimate(
            flops=4 * slots * count * rows * BS * HD * KB,
            bytes_accessed=8 * slots * count * rows * HD,
            transcendentals=slots * count * rows * BS * KB,
        ),
    )(lists, counts, packed)


def give_back(plan, results):
    slots, count, rows, _ = results.shape
    heads = plan.heads

    def body(in_ref, out_ref, landed, sends, recvs, own):
        me = lax.axis_index("blk")

        def remote(slot, hop, head):
            return pltpu.make_async_remote_copy(
                src_ref=in_ref.at[slot, hop],
                dst_ref=landed.at[head],
                send_sem=sends.at[slot, hop],
                recv_sem=recvs.at[head],
                device_id={"blk": (me + count - hop) % count},
                device_id_type=MESH,
            )

        def local(slot, head):
            return pltpu.make_async_copy(in_ref.at[slot, 0], landed.at[head], own.at[slot])

        greet(count)
        first = plan.first_head(me)
        for slot in range(slots):
            for hop in range(count):

                @pl.when(plan.active((me + count - hop) % count, me, slot))
                def _():
                    if hop:
                        remote(slot, hop, first + slot).start()
                    else:
                        local(slot, first + slot).start()

        for slot in range(slots):
            for hop in range(count):

                @pl.when(plan.active((me + count - hop) % count, me, slot))
                def _():
                    if hop:
                        remote(slot, hop, first + slot).wait_send()
                    else:
                        local(slot, first + slot).wait()

        for head in range(heads):

            @pl.when(plan.handler(me, head) != me)
            def _():
                remote(0, 1, head).wait_recv()

            out_ref[:, head * HD : (head + 1) * HD] = landed[head]

    vmem = pl.BlockSpec(memory_space=pltpu.VMEM)
    dma = pltpu.SemaphoreType.DMA
    return pl.pallas_call(
        body,
        out_shape=jax.ShapeDtypeStruct((rows, heads * HD), jnp.bfloat16),
        in_specs=[vmem],
        out_specs=vmem,
        scratch_shapes=[
            pltpu.VMEM((heads, rows, HD), jnp.bfloat16),
            dma((slots, count)),
            dma((heads,)),
            dma((slots,)),
        ],
        compiler_params=pltpu.CompilerParams(
            collective_id=1, has_side_effects=True, vmem_limit_bytes=48 * 1024 * 1024
        ),
        cost_estimate=pl.CostEstimate(
            flops=0, bytes_accessed=8 * heads * rows * HD, transcendentals=0
        ),
    )(results)


def project(attended, out_weight):
    groups = lax.axis_size("head")
    mine = lax.axis_index("head")
    rows = attended.shape[0] // groups
    width = out_weight.shape[1]
    cuts = 4
    piece = width // cuts

    def share(owner, cut):
        return jnp.dot(
            lax.dynamic_slice_in_dim(attended, owner * rows, rows, 0),
            out_weight[:, cut * piece : (cut + 1) * piece],
            preferred_element_type=jnp.float32,
        ).astype(jnp.bfloat16)

    arrived = [
        [
            lax.ppermute(share(mine ^ hop, cut), "head", [(g, g ^ hop) for g in range(groups)])
            for hop in range(1, groups)
        ]
        for cut in range(cuts)
    ]
    done = []
    for cut in range(cuts):
        total = share(mine, cut).astype(jnp.float32)
        for part in arrived[cut]:
            total = total + part.astype(jnp.float32)
        done.append(total.astype(jnp.bfloat16))
    return jnp.concatenate(done, axis=1)


def on_device(queries, keys, values, block_list, block_count, out_weight):
    rows, width = queries.shape
    devices = lax.axis_size("blk")
    me = lax.axis_index("blk")
    plan = Plan(width // HD, devices)
    blocks = rows // BS
    table = jnp.concatenate([block_list, block_count[:, None]], axis=1)
    table = jnp.pad(table, ((0, META - blocks), (0, HD - KB - 1)))
    packed, tables = exchange(plan, queries, keys, values, table)
    tables = tables[:, :blocks].reshape(devices * blocks, HD)
    lists, counts = tables[:, :KB], tables[:, KB].reshape(devices, blocks)
    lists = (me - lists // blocks) % devices * blocks + lists % blocks
    homes = (me - jnp.arange(devices, dtype=jnp.int32)) % devices
    handled = [
        jnp.where(plan.active(homes, me, slot)[:, None], counts, 0).reshape(-1)
        for slot in range(plan.slots)
    ]
    results = attend(plan, lists.reshape(-1), jnp.concatenate(handled), packed)
    return project(give_back(plan, results), out_weight)


def solution(mesh):
    placed = (
        P(("dp", "blk"), "head"),
        P(("dp", "blk"), "head"),
        P(("dp", "blk"), "head"),
        P(("dp", "blk"), None),
        P(("dp", "blk")),
        P("head", None),
    )
    return jax.shard_map(
        on_device,
        mesh=mesh,
        in_specs=placed,
        out_specs=P(("dp", "blk", "head"), None),
        check_vma=False,
    )
```

time: 874 us -> 420 us (0.48)
  starting transfers between devices: 181 us -> 4.05 us
  Pallas kernels: 480 us -> 339 us
  blocking collectives: 68.6 us -> 0 us
  waiting for transfers between devices: 73.9 us -> 22.2 us
  local copies, waits for them, and re-layouts: 37.6 us -> 4.95 us
  matrix products: 27.8 us -> 41.9 us
    ppermute x63 -> x0, starting transfers between devices: 177 us -> none  [the longest x21 71.3 us: on_device(): lax.ppermute(results[hop], 'blk', [(handler, home) for home, handler in p...]
    pallas_call x7 -> x3, Pallas kernels: 480 us -> 339 us  [the longest x1 199 us: exchange(): pl.pallas_call(body, out_shape=[jax.ShapeDtypeStruct((slots, count, 3, ro...]
    all_gather x1 -> x0, blocking collectives: 56.8 us -> none  [on_device(): lists = lax.all_gather(block_list, 'blk', axis=0)[homes]]
    ppermute x63 -> x0, waiting for transfers between devices: 46 us -> none  [the longest x21 25.4 us: on_device(): lax.ppermute(kv_parts[hop], 'blk', [(b, b ^ hop) for b in range(devices)])]
    unnamed x205 -> x5, local copies, waits for them, and re-layouts: 36.1 us -> 3.55 us
    dot_general x8, matrix products: 27.8 us -> 41.9 us  [share(): jnp.dot(lax.dynamic_slice_in_dim(attended, owner * rows, rows, 0), out_we...]
    unnamed x1 -> x0, blocking collectives: 11.8 us -> none
  transfers between devices with their start and end apart: 67 -> 4, of which waited for: 14 -> 3; matrix products, arithmetic and copies ran while one was open for 2% -> 8% of each run, Pallas kernels for 35% -> 0%
where the time goes in v2:
time: 420 us; the launch traced here: 415 us
  Pallas kernels  339 us (81%)
  matrix products  41.9 us (10%)
  waiting for transfers between devices  22.2 us (5%)
  local copies, waits for them, and re-layouts  4.95 us (1%)
    pallas_call x1, Pallas kernels, exchange(): pl.pallas_call(body, out_shape=[jax.ShapeDtypeStruct((slots, count, 3, ro...  199 us
    pallas_call x1, Pallas kernels, attend(): pl.pallas_call(body, grid=(slots,), out_shape=jax.ShapeDtypeStruct((slots...  72.4 us
    pallas_call x1, Pallas kernels, give_back(): pl.pallas_call(body, out_shape=jax.ShapeDtypeStruct((rows, heads * HD), j...  67.5 us
    dot_general x8, matrix products, share(): jnp.dot(lax.dynamic_slice_in_dim(attended, owner * rows, rows, 0), out_we...  41.9 us
    ppermute x4, waiting for transfers between devices, project(): lax.ppermute(share(mine ^ hop, cut), 'head', [(g, g ^ hop) for g in range...  22.2 us
  transfers between devices with their start and end apart: 4, of which 3 were waited for; matrix products, arithmetic and copies ran while one was open for 8% of the time, Pallas kernels for 0%

profile of v2, /device:TPU:10, one launch (start us, length us, event | category | flops | bytes accessed | tf_op | source)
XLA Modules:
  0.0 415.0 jit_solution(15326852703080493748)
XLA Ops:
  0.0 0.7 copy.9
  0.7 0.8 pad_add_fusion
  1.5 1.7 copy-done
  3.2 1.7 copy-done.1
  5.0 199.2 %shard_map.64 = (bf16[3,8,3,512,128]{4,3,2,1,0:T(8,128)(2,1)}, s32[8,8,128]{2,1,0:T(8,128)S(1)}) custom-call(bf16[512,2560]{1,0:T(8,128)(2,1)S(1)} %copy-done, bf16[512,2560]{1,0:T(8,128)(2,1)S(1)} %copy-done.1, bf16[512,2560]{1,0:T(8,128)(2,1)} %v_ref.1, s32[8,128]{1,0:T(8,128)S(1)} %pad.4.t_ref), custom_call_target="tpu_custom_call" | custom-call | bytes 18874368 | tf_op jit(solution)/shard_map/pallas_call | solution.py:126
  204.4 0.1 broadcast_in_dim.40
  204.5 0.1 broadcast_in_dim.41
  204.6 0.1 broadcast_in_dim.42
  204.6 0.1 broadcast_in_dim.43
  204.8 0.1 broadcast_in_dim.37
  204.8 0.1 broadcast_in_dim.38
  204.9 0.1 copy.11
  205.0 0.1 reshape.81.list_ref
  205.1 0.1 pad_add_fusion.1.count_ref
  205.2 72.4 %shard_map.65.in_ref = bf16[3,8,512,128]{3,2,1,0:T(8,128)(2,1)S(1)} custom-call(s32[512]{0:T(512)S(1)} %reshape.81.list_ref, s32[96]{0:T(128)S(1)} %pad_add_fusion.1.count_ref, bf16[3,8,3,512,128]{4,3,2,1,0:T(8,128)(2,1)} %get-tuple-element.8.in_ref), custom_call_target="tpu_custom_call" | custom-call | flops 12884901888 | bytes 12582912 | tf_op jit(solution)/shard_map/pallas_call | solution.py:219
  277.6 67.5 %shard_map.66 = bf16[512,2560]{1,0:T(8,128)(2,1)S(1)} custom-call(bf16[3,8,512,128]{3,2,1,0:T(8,128)(2,1)S(1)} %shard_map.65.in_ref), custom_call_target="tpu_custom_call" | custom-call | bytes 10485760 | tf_op jit(solution)/shard_map/pallas_call | solution.py:291
  345.1 5.6 %fusion.22 = bf16[256,1280]{1,0:T(8,128)(2,1)} fusion(bf16[2560,5120]{1,0:T(8,128)(2,1)} %param.11, bf16[512,2560]{1,0:T(8,128)(2,1)S(1)} %shard_map.66, s32[]{:T(128)S(6)} %select_n.114), kind=kOutput, calls=%fused_computation.19 | convolution fusion | flops 1678049280 | bytes 8519684 | tf_op jit(solution)/shard_map/dot_general | solution.py:320
  350.7 1.5 collective-permute-start
  352.2 5.6 %fusion.31 = bf16[256,1280]{1,0:T(8,128)(2,1)} fusion(bf16[2560,5120]{1,0:T(8,128)(2,1)} %param.11, bf16[512,2560]{1,0:T(8,128)(2,1)S(1)} %shard_map.66, s32[]{:T(128)S(6)} %select_n.114), kind=kOutput, calls=%fused_computation.22 | convolution fusion | flops 1678049280 | bytes 8519684 | tf_op jit(solution)/shard_map/dot_general | solution.py:320
  357.8 0.5 collective-permute-start.1
  358.3 5.6 %fusion.40 = bf16[256,1280]{1,0:T(8,128)(2,1)} fusion(bf16[2560,5120]{1,0:T(8,128)(2,1)} %param.11, bf16[512,2560]{1,0:T(8,128)(2,1)S(1)} %shard_map.66, s32[]{:T(128)S(6)} %select_n.114), kind=kOutput, calls=%fused_computation.25 | convolution fusion | flops 1678049280 | bytes 8519684 | tf_op jit(solution)/shard_map/dot_general | solution.py:320
  363.9 1.5 collective-permute-start.2
  365.4 5.6 %fusion.49 = bf16[256,1280]{1,0:T(8,128)(2,1)} fusion(bf16[2560,5120]{1,0:T(8,128)(2,1)} %param.11, bf16[512,2560]{1,0:T(8,128)(2,1)S(1)} %shard_map.66, s32[]{:T(128)S(6)} %select_n.114), kind=kOutput, calls=%fused_computation.28 | convolution fusion | flops 1678049280 | bytes 8519684 | tf_op jit(solution)/shard_map/dot_general | solution.py:320
  371.0 0.5 collective-permute-start.3
  371.5 4.9 %add_convert_fusion.3 = bf16[256,1280]{1,0:T(8,128)(2,1)S(1)} fusion(bf16[256,1280]{1,0:T(8,128)(2,1)} %collective-permute-done, bf16[2560,5120]{1,0:T(8,128)(2,1)} %param.11, bf16[512,2560]{1,0:T(8,128)(2,1)S(1)} %shard_map.66, s32[]{:T(128)S(6)} %select_n.113), kind=kOutput, calls=%fused_computation.32 | convolution fusion | flops 1679360000 | bytes 9175044 | tf_op jit(solution)/shard_map/dot_general | solution.py:320
  376.4 6.3 %collective-permute-done.1 = bf16[256,1280]{1,0:T(8,128)(2,1)} collective-permute-done((bf16[256,1280]{1,0:T(8,128)(2,1)}, bf16[256,1280]{1,0:T(8,128)(2,1)}, u32[]{:S(2)}, u32[]{:S(2)}) %collective-permute-start.1) | collective-permute-done | bytes 655392 | tf_op jit(solution)/shard_map/ppermute | solution.py:328
  382.7 4.9 %add_convert_fusion.2 = bf16[256,1280]{1,0:T(8,128)(2,1)S(1)} fusion(bf16[256,1280]{1,0:T(8,128)(2,1)} %collective-permute-done.1, bf16[2560,5120]{1,0:T(8,128)(2,1)} %param.11, bf16[512,2560]{1,0:T(8,128)(2,1)S(1)} %shard_map.66, s32[]{:T(128)S(6)} %select_n.113), kind=kOutput, calls=%fused_computation.31 | convolution fusion | flops 1679360000 | bytes 9175044 | tf_op jit(solution)/shard_map/dot_general | solution.py:320
  387.6 9.1 %collective-permute-done.2 = bf16[256,1280]{1,0:T(8,128)(2,1)} collective-permute-done((bf16[256,1280]{1,0:T(8,128)(2,1)}, bf16[256,1280]{1,0:T(8,128)(2,1)}, u32[]{:S(2)}, u32[]{:S(2)}) %collective-permute-start.2) | collective-permute-done | bytes 655392 | tf_op jit(solution)/shard_map/ppermute | solution.py:328
  396.8 5.0 %add_convert_fusion.1 = bf16[256,1280]{1,0:T(8,128)(2,1)S(1)} fusion(bf16[256,1280]{1,0:T(8,128)(2,1)} %collective-permute-done.2, bf16[2560,5120]{1,0:T(8,128)(2,1)} %param.11, bf16[512,2560]{1,0:T(8,128)(2,1)S(1)} %shard_map.66, s32[]{:T(128)S(6)} %select_n.113), kind=kOutput, calls=%fused_computation.30 | convolution fusion | flops 1679360000 | bytes 9175044 | tf_op jit(solution)/shard_map/dot_general | solution.py:320
  401.7 6.8 %collective-permute-done.3 = bf16[256,1280]{1,0:T(8,128)(2,1)S(1)} collective-permute-done((bf16[256,1280]{1,0:T(8,128)(2,1)}, bf16[256,1280]{1,0:T(8,128)(2,1)S(1)}, u32[]{:S(2)}, u32[]{:S(2)}) %collective-permute-start.3) | collective-permute-done | bytes 655392 | tf_op jit(solution)/shard_map/ppermute | solution.py:328
  408.5 4.8 %add_convert_fusion = bf16[256,1280]{1,0:T(8,128)(2,1)S(1)} fusion(bf16[256,1280]{1,0:T(8,128)(2,1)S(1)} %collective-permute-done.3, bf16[2560,5120]{1,0:T(8,128)(2,1)} %param.11, bf16[512,2560]{1,0:T(8,128)(2,1)S(1)} %shard_map.66, s32[]{:T(128)S(6)} %select_n.113), kind=kOutput, calls=%fused_computation.29 | convolution fusion | flops 1679360000 | bytes 9175044 | tf_op jit(solution)/shard_map/dot_general | solution.py:320
  413.3 1.6 pad_maximum_fusion
  (10 shorter events, 0.2 us)
Async XLA Ops:
  1.5 1.7 copy-start
  3.2 1.7 copy-start.1
  350.7 20.8 %collective-permute-start = (bf16[256,1280]{1,0:T(8,128)(2,1)}, bf16[256,1280]{1,0:T(8,128)(2,1)}, u32[]{:S(2)}, u32[]{:S(2)}) collective-permute-start(bf16[256,1280]{1,0:T(8,128)(2,1)} %fusion.22), channel_id=1, source_target_pairs={{0,1},{1,0},{2,3},{3,2},{4,5},{5,4},{6,7},{7,6},{8,9},{9,8},{10,11... | collective-permute-start | bytes 1966088 | tf_op jit(solution)/shard_map/ppermute | solution.py:328
  357.8 24.9 %collective-permute-start.1 = (bf16[256,1280]{1,0:T(8,128)(2,1)}, bf16[256,1280]{1,0:T(8,128)(2,1)}, u32[]{:S(2)}, u32[]{:S(2)}) collective-permute-start(bf16[256,1280]{1,0:T(8,128)(2,1)} %fusion.31), channel_id=1, source_target_pairs={{0,1},{1,0},{2,3},{3,2},{4,5},{5,4},{6,7},{7,6},{8,9},{9,8},{10,11... | collective-permute-start | bytes 1966088 | tf_op jit(solution)/shard_map/ppermute | solution.py:328
  363.9 32.9 %collective-permute-start.2 = (bf16[256,1280]{1,0:T(8,128)(2,1)}, bf16[256,1280]{1,0:T(8,128)(2,1)}, u32[]{:S(2)}, u32[]{:S(2)}) collective-permute-start(bf16[256,1280]{1,0:T(8,128)(2,1)} %fusion.40), channel_id=1, source_target_pairs={{0,1},{1,0},{2,3},{3,2},{4,5},{5,4},{6,7},{7,6},{8,9},{9,8},{10,11... | collective-permute-start | bytes 1966088 | tf_op jit(solution)/shard_map/ppermute | solution.py:328
  371.0 37.6 %collective-permute-start.3 = (bf16[256,1280]{1,0:T(8,128)(2,1)}, bf16[256,1280]{1,0:T(8,128)(2,1)S(1)}, u32[]{:S(2)}, u32[]{:S(2)}) collective-permute-start(bf16[256,1280]{1,0:T(8,128)(2,1)} %fusion.49), channel_id=1, source_target_pairs={{0,1},{1,0},{2,3},{3,2},{4,5},{5,4},{6,7},{7,6},{8,9},{9,8},{10,11... | collective-permute-start | bytes 1966088 | tf_op jit(solution)/shard_map/ppermute | solution.py:328

commit v3 on v0

v3 whole, which is shorter than its diff:
```python
import functools
import math

import jax
import jax.numpy as jnp
from jax import lax
from jax.experimental import pallas as pl
from jax.experimental.pallas import tpu as pltpu
from jax.sharding import PartitionSpec as P

HD = 128
BS = 128
KB = 16
META = 8
MESH = pl.DeviceIdType.MESH


class Plan:
    def __init__(self, heads, devices):
        self.heads, self.devices = heads, devices
        self.parts = 1
        while heads * self.parts % devices:
            self.parts *= 2
        self.each = heads * self.parts // devices
        firsts = [self.each * b // self.parts for b in range(devices)]
        lasts = [(self.each * b + self.each - 1) // self.parts for b in range(devices)]
        self.slots = max(last - first + 1 for first, last in zip(firsts, lasts))
        self.clipped = max(firsts) > heads - self.slots

    def head_of(self, handler, phase):
        first = handler * self.each // self.parts
        if self.clipped:
            first = jnp.minimum(first, self.heads - self.slots)
        late = (handler * self.each % self.parts + self.parts - 1) // self.parts
        return first + (phase + late) % self.slots

    def handler(self, home, head):
        return (head * self.parts + home * self.parts // self.devices) // self.each

    def active(self, home, handler, phase):
        return self.handler(home, self.head_of(handler, phase)) == handler


def greet(count):
    me = lax.axis_index("blk")
    barrier = pltpu.get_barrier_semaphore()
    for hop in range(1, count):
        pl.semaphore_signal(
            barrier, inc=1, device_id={"blk": (me + hop) % count}, device_id_type=MESH
        )
    pl.semaphore_wait(barrier, count - 1)


def attention(plan, queries, keys, values, table):
    rows = queries.shape[0]
    blocks = rows // BS
    count, phases, heads = plan.devices, plan.slots, plan.heads
    factor = math.log2(math.e) / math.sqrt(HD)
    side = 2 if blocks % 2 == 0 else 1

    def body(
        q_ref, k_ref, v_ref, t_ref, out_ref,
        held, results, landed, tables, lists, scores_ref,
        sends, recvs, t_sends, t_recvs, back_sends, back_recvs, own, *got,
    ):
        me = lax.axis_index("blk")

        def big(phase, hop, both):
            part = pl.ds(0, 2) if both else pl.ds(2, 1)
            which = 0 if both else 1
            return pltpu.make_async_remote_copy(
                src_ref=held.at[phase, hop, part],
                dst_ref=got[phase].at[hop, part],
                send_sem=sends.at[phase, hop, which],
                recv_sem=recvs.at[phase, hop, which],
                device_id={"blk": (me + hop) % count},
                device_id_type=MESH,
            )

        def small(hop):
            return pltpu.make_async_remote_copy(
                src_ref=t_ref,
                dst_ref=tables.at[hop],
                send_sem=t_sends.at[hop],
                recv_sem=t_recvs.at[hop],
                device_id={"blk": (me + hop) % count},
                device_id_type=MESH,
            )

        def back(phase, hop, head):
            return pltpu.make_async_remote_copy(
                src_ref=results.at[phase, hop],
                dst_ref=landed.at[head],
                send_sem=back_sends.at[phase, hop],
                recv_sem=back_recvs.at[head],
                device_id={"blk": (me + count - hop) % count},
                device_id_type=MESH,
            )

        def stay(phase, head):
            return pltpu.make_async_copy(results.at[phase, 0], landed.at[head], own.at[phase])

        far_first = sorted(range(1, count), key=lambda hop: -min(hop, count - hop))

        def send(phase):
            for hop in far_first + [0]:
                handler = (me + hop) % count
                head = plan.head_of(handler, phase)
                columns = pl.ds(pl.multiple_of(head * HD, HD), HD)
                into = held.at[phase, hop] if hop else got[phase].at[0]
                into[0] = k_ref[:, columns].reshape(blocks, BS, HD)
                into[1] = v_ref[:, columns].reshape(blocks, BS, HD)
                into[2] = q_ref[:, columns].reshape(blocks, BS, HD)
                if hop:
                    big(phase, hop, True).start()

                    @pl.when(plan.active(me, handler, phase))
                    def _():
                        big(phase, hop, False).start()

        def arrive(phase):
            for hop in range(1, count):
                big(phase, hop, True).wait_recv()

                @pl.when(plan.active((me + count - hop) % count, me, phase))
                def _():
                    big(phase, hop, False).wait_recv()

        def attend_block(phase, hop, block, lane):
            query = got[phase][hop, 2, block]
            used = lists[hop, block, KB]
            places = []
            for j in range(KB):
                at = lists[hop, block, j]
                source = lax.rem(me - lax.div(at, blocks) + count, count)
                places.append((source, lax.rem(at, blocks)))

            def listed(j, kind):
                pair = [got[phase][source, kind, block] for source, block in places[j : j + 2]]
                return jnp.concatenate(pair, axis=0)

            highest = None
            for j in range(0, KB, 2):
                pair = lax.dot_general(
                    query, listed(j, 0), (((1,), (1,)), ((), ())), preferred_element_type=jnp.float32
                )
                for n in range(2):
                    scores = pair[:, n * BS : (n + 1) * BS]
                    if j + n >= 4:
                        unused = jnp.minimum(used - (j + n + 1), 0).astype(jnp.float32)
                        scores = scores + unused * 1e30
                    scores_ref[lane, j + n] = scores
                    highest = scores if highest is None else jnp.maximum(highest, scores)
            highest = jnp.max(highest, axis=1, keepdims=True)
            total = jnp.zeros((BS, BS), jnp.float32)
            mixed = jnp.zeros((BS, HD), jnp.float32)
            for j in range(0, KB, 2):
                pair = []
                for n in range(2):
                    weights = jnp.exp2((scores_ref[lane, j + n] - highest) * factor)
                    total = total + weights
                    pair.append(weights.astype(jnp.bfloat16))
                mixed = mixed + jnp.dot(
                    jnp.concatenate(pair, axis=1), listed(j, 1), preferred_element_type=jnp.float32
                )
            total = jnp.sum(total, axis=1, keepdims=True)
            results[phase, hop, pl.ds(pl.multiple_of(block * BS, BS), BS), :] = (
                mixed / total
            ).astype(jnp.bfloat16)

        def attend(phase):
            head = plan.head_of(me, phase)

            def one_home(turn, carry):
                hop = count - 1 - turn

                @pl.when(plan.active((me + count - hop) % count, me, phase))
                def _():
                    def some(i, carry):
                        for lane in range(side):
                            attend_block(phase, hop, i * side + lane, lane)
                        return carry

                    lax.fori_loop(0, blocks // side, some, 0)

                    @pl.when(hop > 0)
                    def _():
                        back(phase, hop, head).start()

                    @pl.when(hop == 0)
                    def _():
                        stay(phase, head).start()

                return carry

            lax.fori_loop(0, count, one_home, 0)

        greet(count)
        for hop in range(1, count):
            small(hop).start()
        tables[0] = t_ref[...]
        for phase in range(min(2, phases)):
            send(phase)
        for hop in range(1, count):
            small(hop).wait()
        to_scalar = pltpu.make_async_copy(tables, lists, own.at[phases])
        to_scalar.start()
        to_scalar.wait()

        for phase in range(phases):
            arrive(phase)
            if phase + 2 < phases:
                send(phase + 2)
            attend(phase)

        for phase in range(phases):
            for hop in range(1, count):
                big(phase, hop, True).wait_send()

                @pl.when(plan.active(me, (me + hop) % count, phase))
                def _():
                    big(phase, hop, False).wait_send()

            for hop in range(count):

                @pl.when(plan.active((me + count - hop) % count, me, phase))
                def _():
                    if hop:
                        back(phase, hop, plan.head_of(me, phase)).wait_send()
                    else:
                        stay(phase, plan.head_of(me, phase)).wait()

        for head in range(heads):

            @pl.when(plan.handler(me, head) != me)
            def _():
                back(0, 1, head).wait_recv()

            out_ref[:, head * HD : (head + 1) * HD] = landed[head]

    vmem = pl.BlockSpec(memory_space=pltpu.VMEM)
    dma = pltpu.SemaphoreType.DMA
    kind = queries.dtype
    return pl.pallas_call(
        body,
        out_shape=jax.ShapeDtypeStruct((rows, heads * HD), kind),
        in_specs=[vmem] * 4,
        out_specs=vmem,
        scratch_shapes=[
            pltpu.VMEM((phases, count, 3, blocks, BS, HD), kind),
            pltpu.VMEM((phases, count, rows, HD), kind),
            pltpu.VMEM((heads, rows, HD), kind),
            pltpu.VMEM((count, META, HD), jnp.int32),
            pltpu.SMEM((count, META, HD), jnp.int32),
            pltpu.VMEM((side, KB, BS, BS), jnp.float32),
            dma((phases, count, 2)),
            dma((phases, count, 2)),
            dma((count,)),
            dma((count,)),
            dma((phases, count)),
            dma((heads,)),
            dma((phases + 1,)),
        ]
        + [pltpu.VMEM((count, 3, blocks, BS, HD), kind)] * phases,
        compiler_params=pltpu.CompilerParams(
            collective_id=0, has_side_effects=True, vmem_limit_bytes=56 * 1024 * 1024
        ),
        cost_estimate=pl.CostEstimate(
            flops=4 * heads * rows * BS * HD * KB,
            bytes_accessed=8 * heads * rows * HD,
            transcendentals=heads * rows * BS * KB,
        ),
    )(queries, keys, values, table)


def project(attended, out_weight):
    groups = lax.axis_size("head")
    mine = lax.axis_index("head")
    rows = attended.shape[0] // groups
    width = out_weight.shape[1]
    cuts = 4
    piece = width // cuts

    def share(owner, cut):
        return jnp.dot(
            lax.dynamic_slice_in_dim(attended, owner * rows, rows, 0),
            out_weight[:, cut * piece : (cut + 1) * piece],
            preferred_element_type=jnp.float32,
        ).astype(jnp.bfloat16)

    arrived = [
        [
            lax.ppermute(share(mine ^ hop, cut), "head", [(g, g ^ hop) for g in range(groups)])
            for hop in range(1, groups)
        ]
        for cut in range(cuts)
    ]
    done = []
    for cut in range(cuts):
        total = share(mine, cut).astype(jnp.float32)
        for part in arrived[cut]:
            total = total + part.astype(jnp.float32)
        done.append(total.astype(jnp.bfloat16))
    return jnp.concatenate(done, axis=1)


def on_device(queries, keys, values, block_list, block_count, out_weight):
    rows, width = queries.shape
    devices = lax.axis_size("blk")
    plan = Plan(width // HD, devices)
    blocks = rows // BS
    table = jnp.concatenate([block_list, block_count[:, None]], axis=1)
    table = jnp.pad(table, ((0, META - blocks), (0, HD - KB - 1)))
    return project(attention(plan, queries, keys, values, table), out_weight)


def solution(mesh):
    placed = (
        P(("dp", "blk"), "head"),
        P(("dp", "blk"), "head"),
        P(("dp", "blk"), "head"),
        P(("dp", "blk"), None),
        P(("dp", "blk")),
        P("head", None),
    )
    return jax.shard_map(
        on_device,
        mesh=mesh,
        in_specs=placed,
        out_specs=P(("dp", "blk", "head"), None),
        check_vma=False,
    )
```

time: 1330 us -> 345 us (0.26)
  waiting for transfers between devices: 869 us -> 27.9 us
  Pallas kernels: 0 us -> 271 us
  matrix products: 237 us -> 37.7 us
  local copies, waits for them, and re-layouts: 118 us -> 1.35 us
  other arithmetic: 88.1 us -> 2.4 us
    all_gather x2 -> x0, waiting for transfers between devices: 800 us -> none  [the longest x1 403 us: on_device(): value_piece = lax.all_gather(values, 'blk', axis=0, tiled=True)]
    pallas_call x0 -> x1, Pallas kernels: none -> 271 us  [attention(): pl.pallas_call(body, out_shape=jax.ShapeDtypeStruct((rows, heads * HD), k...]
    dot_general x25 -> x8, matrix products: 237 us -> 37.7 us  [share(): jnp.dot(lax.dynamic_slice_in_dim(attended, owner * rows, rows, 0), out_we...]
    dynamic_slice x32 -> x0, local copies, waits for them, and re-layouts: 96.7 us -> none  [on_device(): lax.scan(advance, initial, (key_split, value_split, offsets))]
    reduce_sum x9 -> x0, other arithmetic: 78.8 us -> none  [the longest x8 78.7 us: attend(): totals = totals * rescale + jnp.sum(weights, axis=-1)]
    reduce_scatter x1 -> x0, waiting for transfers between devices: 66.8 us -> none  [on_device(): lax.psum_scatter(jnp.dot(attended, out_weight, preferred_element_type=jnp...]
    ppermute x0 -> x4, waiting for transfers between devices: none -> 27.9 us  [project(): lax.ppermute(share(mine ^ hop, cut), 'head', [(g, g ^ hop) for g in range...]
  transfers between devices with their start and end apart: 3 -> 4, of which waited for: 3 -> 4; matrix products, arithmetic and copies ran while one was open for 0% -> 8% of each run, Pallas kernels for 0% -> 0%
where the time goes in v3:
time: 345 us
  Pallas kernels  271 us (79%)
  matrix products  37.7 us (11%)
  waiting for transfers between devices  27.9 us (8%)
  starting transfers between devices  4.18 us (1%)
    pallas_call x1, Pallas kernels, attention(): pl.pallas_call(body, out_shape=jax.ShapeDtypeStruct((rows, heads * HD), k...  271 us
    dot_general x8, matrix products, share(): jnp.dot(lax.dynamic_slice_in_dim(attended, owner * rows, rows, 0), out_we...  37.7 us
    ppermute x4, waiting for transfers between devices, project(): lax.ppermute(share(mine ^ hop, cut), 'head', [(g, g ^ hop) for g in range...  27.9 us
  transfers between devices with their start and end apart: 4, of which 4 were waited for; matrix products, arithmetic and copies ran while one was open for 8% of the time, Pallas kernels for 0%

profile of v3, /device:TPU:10, one launch (start us, length us, event | category | flops | bytes accessed | tf_op | source)
XLA Modules:
  0.0 344.8 jit_solution(14359733405624148669)
XLA Ops:
  0.0 0.7 copy.7
  0.7 0.8 pad_add_fusion
  1.5 0.6 pad.4.t_ref
  2.1 271.3 %shard_map.64 = bf16[512,2560]{1,0:T(8,128)(2,1)} custom-call(bf16[512,2560]{1,0:T(8,128)(2,1)} %q_ref.1, bf16[512,2560]{1,0:T(8,128)(2,1)} %k_ref.1, bf16[512,2560]{1,0:T(8,128)(2,1)} %v_ref.1, s32[8,128]{1,0:T(8,128)} %pad.4.t_ref), custom_call_target="tpu_custom_call" | custom-call | flops 10737418240 | bytes 10485760 | tf_op jit(solution)/shard_map/pallas_call | solution.py:244
  273.4 0.0 copy-start
  273.4 6.1 %fusion.22 = bf16[256,1280]{1,0:T(8,128)(2,1)} fusion(bf16[2560,5120]{1,0:T(8,128)(2,1)} %param.11, bf16[512,2560]{1,0:T(8,128)(2,1)} %shard_map.64, s32[]{:T(128)S(6)} %select_n.5), kind=kOutput, calls=%fused_computation.19 | convolution fusion | flops 1678049280 | bytes 8519684 | tf_op jit(solution)/shard_map/dot_general | solution.py:285
  279.5 1.5 collective-permute-start
  281.0 6.7 %fusion.49 = bf16[256,1280]{1,0:T(8,128)(2,1)} fusion(bf16[2560,5120]{1,0:T(8,128)(2,1)} %param.11, bf16[512,2560]{1,0:T(8,128)(2,1)} %shard_map.64, s32[]{:T(128)S(6)} %select_n.5), kind=kOutput, calls=%fused_computation.28 | convolution fusion | flops 1678049280 | bytes 8519684 | tf_op jit(solution)/shard_map/dot_general | solution.py:285
  287.7 0.0 copy-start.1
  287.7 0.5 collective-permute-start.3
  288.2 0.0 copy-done
  288.2 3.4 fusion.40
  291.7 1.3 collective-permute-start.2
  293.0 0.0 copy-done.1
  293.0 1.9 fusion.31
  294.9 0.8 collective-permute-start.1
  295.7 0.0 copy-start.2
  295.7 1.7 collective-permute-done
  297.4 5.4 %add_convert_fusion.3 = bf16[256,1280]{1,0:T(8,128)(2,1)S(1)} fusion(bf16[256,1280]{1,0:T(8,128)(2,1)} %collective-permute-done, bf16[2560,5120]{1,0:T(8,128)(2,1)} %param.11, bf16[512,2560]{1,0:T(8,128)(2,1)} %shard_map.64, s32[]{:T(128)S(6)} %select_n.4), kind=kOutput, calls=%fused_computation.32 | convolution fusion | flops 1679360000 | bytes 9175044 | tf_op jit(solution)/shard_map/dot_general | solution.py:285
  302.8 8.6 %collective-permute-done.3 = bf16[256,1280]{1,0:T(8,128)(2,1)S(1)} collective-permute-done((bf16[256,1280]{1,0:T(8,128)(2,1)}, bf16[256,1280]{1,0:T(8,128)(2,1)S(1)}, u32[]{:S(2)}, u32[]{:S(2)}) %collective-permute-start.3) | collective-permute-done | bytes 655392 | tf_op jit(solution)/shard_map/ppermute | solution.py:293
  311.4 0.0 copy-done.2
  311.4 4.8 %add_convert_fusion = bf16[256,1280]{1,0:T(8,128)(2,1)S(1)} fusion(bf16[256,1280]{1,0:T(8,128)(2,1)S(1)} %collective-permute-done.3, bf16[2560,5120]{1,0:T(8,128)(2,1)} %param.11, bf16[512,2560]{1,0:T(8,128)(2,1)S(1)} %copy-done.2, s32[]{:T(128)S(6)} %select_n.4), kind=kOutput, calls=%fused_computation.29 | convolution fusion | flops 1679360000 | bytes 9175044 | tf_op jit(solution)/shard_map/dot_general | solution.py:285
  316.1 9.3 %collective-permute-done.2 = bf16[256,1280]{1,0:T(8,128)(2,1)S(1)} collective-permute-done((bf16[256,1280]{1,0:T(8,128)(2,1)S(1)}, bf16[256,1280]{1,0:T(8,128)(2,1)S(1)}, u32[]{:S(2)}, u32[]{:S(2)}) %collective-permute-start.2) | collective-permute-done | bytes 655392 | tf_op jit(solution)/shard_map/ppermute | solution.py:293
  325.4 4.7 %add_convert_fusion.1 = bf16[256,1280]{1,0:T(8,128)(2,1)S(1)} fusion(bf16[256,1280]{1,0:T(8,128)(2,1)S(1)} %collective-permute-done.2, bf16[2560,5120]{1,0:T(8,128)(2,1)} %param.11, bf16[512,2560]{1,0:T(8,128)(2,1)S(1)} %copy-done.2, s32[]{:T(128)S(6)} %select_n.4), kind=kOutput, calls=%fused_computation.30 | convolution fusion | flops 1679360000 | bytes 9175044 | tf_op jit(solution)/shard_map/dot_general | solution.py:285
  330.2 8.3 %collective-permute-done.1 = bf16[256,1280]{1,0:T(8,128)(2,1)S(1)} collective-permute-done((bf16[256,1280]{1,0:T(8,128)(2,1)S(1)}, bf16[256,1280]{1,0:T(8,128)(2,1)S(1)}, u32[]{:S(2)}, u32[]{:S(2)}) %collective-permute-start.1) | collective-permute-done | bytes 655392 | tf_op jit(solution)/shard_map/ppermute | solution.py:293
  338.5 4.7 %add_convert_fusion.2 = bf16[256,1280]{1,0:T(8,128)(2,1)S(1)} fusion(bf16[256,1280]{1,0:T(8,128)(2,1)S(1)} %collective-permute-done.1, bf16[2560,5120]{1,0:T(8,128)(2,1)} %param.11, bf16[512,2560]{1,0:T(8,128)(2,1)S(1)} %copy-done.2, s32[]{:T(128)S(6)} %select_n.4), kind=kOutput, calls=%fused_computation.31 | convolution fusion | flops 1679360000 | bytes 9175044 | tf_op jit(solution)/shard_map/dot_general | solution.py:285
  343.2 1.6 pad_maximum_fusion
Async XLA Ops:
  273.4 14.8 %copy-start = (bf16[2560,5120]{1,0:T(8,128)(2,1)S(1)}, bf16[2560,5120]{1,0:T(8,128)(2,1)}, u32[]{:S(2)}) copy-start(bf16[2560,5120]{1,0:T(8,128)(2,1)} %param.11) | copy-start | bytes 78643200
  279.5 17.9 %collective-permute-start = (bf16[256,1280]{1,0:T(8,128)(2,1)}, bf16[256,1280]{1,0:T(8,128)(2,1)}, u32[]{:S(2)}, u32[]{:S(2)}) collective-permute-start(bf16[256,1280]{1,0:T(8,128)(2,1)} %fusion.22), channel_id=1, source_target_pairs={{0,1},{1,0},{2,3},{3,2},{4,5},{5,4},{6,7},{7,6},{8,9},{9,8},{10,11... | collective-permute-start | bytes 1966088 | tf_op jit(solution)/shard_map/ppermute | solution.py:293
  287.7 5.3 %copy-start.1 = (bf16[512,2560]{1,0:T(8,128)(2,1)S(1)}, bf16[512,2560]{1,0:T(8,128)(2,1)}, u32[]{:S(2)}) copy-start(bf16[512,2560]{1,0:T(8,128)(2,1)} %shard_map.64) | copy-start | bytes 7864324
  287.7 23.6 %collective-permute-start.3 = (bf16[256,1280]{1,0:T(8,128)(2,1)}, bf16[256,1280]{1,0:T(8,128)(2,1)S(1)}, u32[]{:S(2)}, u32[]{:S(2)}) collective-permute-start(bf16[256,1280]{1,0:T(8,128)(2,1)} %fusion.49), channel_id=1, source_target_pairs={{0,1},{1,0},{2,3},{3,2},{4,5},{5,4},{6,7},{7,6},{8,9},{9,8},{10,11... | collective-permute-start | bytes 1966088 | tf_op jit(solution)/shard_map/ppermute | solution.py:293
  291.7 33.7 %collective-permute-start.2 = (bf16[256,1280]{1,0:T(8,128)(2,1)S(1)}, bf16[256,1280]{1,0:T(8,128)(2,1)S(1)}, u32[]{:S(2)}, u32[]{:S(2)}) collective-permute-start(bf16[256,1280]{1,0:T(8,128)(2,1)S(1)} %fusion.40), channel_id=1, source_target_pairs={{0,1},{1,0},{2,3},{3,2},{4,5},{5,4},{6,7},{7,6},{8,9},{9,8},{10,11... | collective-permute-start | bytes 1966088 | tf_op jit(solution)/shard_map/ppermute | solution.py:293
  294.9 43.6 %collective-permute-start.1 = (bf16[256,1280]{1,0:T(8,128)(2,1)S(1)}, bf16[256,1280]{1,0:T(8,128)(2,1)S(1)}, u32[]{:S(2)}, u32[]{:S(2)}) collective-permute-start(bf16[256,1280]{1,0:T(8,128)(2,1)S(1)} %fusion.31), channel_id=1, source_target_pairs={{0,1},{1,0},{2,3},{3,2},{4,5},{5,4},{6,7},{7,6},{8,9},{9,8},{10,11... | collective-permute-start | bytes 1966088 | tf_op jit(solution)/shard_map/ppermute | solution.py:293
  295.7 15.7 %copy-start.2 = (bf16[512,2560]{1,0:T(8,128)(2,1)S(1)}, bf16[512,2560]{1,0:T(8,128)(2,1)}, u32[]{:S(2)}) copy-start(bf16[512,2560]{1,0:T(8,128)(2,1)} %shard_map.64) | copy-start | bytes 7864324

commit v4 on v3

--- a/solution.py
+++ b/solution.py
@@ -12,6 +12,8 @@
 BS = 128
 KB = 16
 META = 8
+CHUNKS = 5
+FETCHED = 3
 MESH = pl.DeviceIdType.MESH
 
 
@@ -41,29 +43,40 @@
         return self.handler(home, self.head_of(handler, phase)) == handler
 
 
-def greet(count):
-    me = lax.axis_index("blk")
+def greet(count, groups):
+    me, group, core = (lax.axis_index(name) for name in ("blk", "head", "dp"))
     barrier = pltpu.get_barrier_semaphore()
-    for hop in range(1, count):
-        pl.semaphore_signal(
-            barrier, inc=1, device_id={"blk": (me + hop) % count}, device_id_type=MESH
-        )
-    pl.semaphore_wait(barrier, count - 1)
-
-
-def attention(plan, queries, keys, values, table):
+    for hop in range(count):
+        for over in range(groups):
+            if hop or over:
+                pl.semaphore_signal(
+                    barrier,
+                    inc=1,
+                    device_id={"blk": (me + hop) % count, "head": (group + over) % groups},
+                    device_id_type=MESH,
+                )
+    pl.semaphore_signal(barrier, inc=1, device_id={"dp": 1 - core}, device_id_type=MESH)
+    pl.semaphore_wait(barrier, count * groups)
+
+
+def attention(plan, queries, keys, values, table, out_weight):
     rows = queries.shape[0]
     blocks = rows // BS
     count, phases, heads = plan.devices, plan.slots, plan.heads
+    groups = lax.axis_size("head")
+    share = rows // groups
+    chunk_rows = out_weight.shape[0] // (2 * CHUNKS)
     factor = math.log2(math.e) / math.sqrt(HD)
     side = 2 if blocks % 2 == 0 else 1
 
     def body(
-        q_ref, k_ref, v_ref, t_ref, out_ref,
+        q_ref, k_ref, v_ref, t_ref, w_ref, out_ref, w_out,
         held, results, landed, tables, lists, scores_ref,
-        sends, recvs, t_sends, t_recvs, back_sends, back_recvs, own, *got,
+        sends, recvs, t_sends, t_recvs, back_sends, back_recvs, own,
+        y_sends, y_recvs, x_sends, x_recvs, core_sends, core_recvs, *got,
     ):
-        me = lax.axis_index("blk")
+        me, group, core = (lax.axis_index(name) for name in ("blk", "head", "dp"))
+        odd = me % 2
 
         def big(phase, hop, both):
             part = pl.ds(0, 2) if both else pl.ds(2, 1)
@@ -87,18 +100,65 @@
                 device_id_type=MESH,
             )
 
-        def back(phase, hop, head):
-            return pltpu.make_async_remote_copy(
-                src_ref=results.at[phase, hop],
-                dst_ref=landed.at[head],
-                send_sem=back_sends.at[phase, hop],
-                recv_sem=back_recvs.at[head],
-                device_id={"blk": (me + count - hop) % count},
+        def back(phase, hop, over, head):
+            owner = (group + over) % groups
+            return pltpu.make_async_remote_copy(
+                src_ref=results.at[phase, hop, owner],
+                dst_ref=landed.at[over, head],
+                send_sem=back_sends.at[phase, hop, over],
+                recv_sem=back_recvs.at[over, head],
+                device_id={"blk": (me + count - hop) % count, "head": owner},
                 device_id_type=MESH,
             )
 
         def stay(phase, head):
-            return pltpu.make_async_copy(results.at[phase, 0], landed.at[head], own.at[phase])
+            return pltpu.make_async_copy(
+                results.at[phase, 0, group], landed.at[0, head], own.at[phase]
+            )
+
+        def chunk(i, side_x):
+            place = core * CHUNKS + i + side_x * (CHUNKS - 1 - 2 * i)
+            return pl.ds(pl.multiple_of(place * chunk_rows, chunk_rows), chunk_rows)
+
+        def over_y(over, i):
+            return pltpu.make_async_remote_copy(
+                src_ref=w_ref.at[chunk(i, odd)],
+                dst_ref=w_out.at[over - 1, chunk(i, odd)],
+                send_sem=y_sends.at[over - 1, i],
+                recv_sem=y_recvs.at[over - 1, i],
+                device_id={"head": (group + over) % groups},
+                device_id_type=MESH,
+            )
+
+        def over_x(over, i):
+            return pltpu.make_async_remote_copy(
+                src_ref=w_out.at[over - 1, chunk(i, odd)],
+                dst_ref=w_out.at[over - 1, chunk(i, odd)],
+                send_sem=x_sends.at[over - 1, i],
+                recv_sem=x_recvs.at[over - 1, i],
+                device_id={"blk": me + 1 - 2 * odd},
+                device_id_type=MESH,
+            )
+
+        def over_core(over, i):
+            return pltpu.make_async_remote_copy(
+                src_ref=w_out.at[over - 1, chunk(i, odd)],
+                dst_ref=w_out.at[over - 1, chunk(i, odd)],
+                send_sem=core_sends.at[over - 1, i],
+                recv_sem=core_recvs.at[over - 1, i],
+                device_id={"dp": 1 - core},
+                device_id_type=MESH,
+            )
+
+        def pass_on(i):
+            for over in range(1, groups):
+                if i < FETCHED:
+                    over_y(over, i).wait_recv()
+                    if i < CHUNKS - FETCHED:
+                        over_x(over, i).start()
+                else:
+                    over_x(over, CHUNKS - 1 - i).wait_recv()
+                over_core(over, i).start()
 
         far_first = sorted(range(1, count), key=lambda hop: -min(hop, count - hop))
 
@@ -164,9 +224,14 @@
                     jnp.concatenate(pair, axis=1), listed(j, 1), preferred_element_type=jnp.float32
                 )
             total = jnp.sum(total, axis=1, keepdims=True)
-            results[phase, hop, pl.ds(pl.multiple_of(block * BS, BS), BS), :] = (
-                mixed / total
-            ).astype(jnp.bfloat16)
+            mixed = (mixed / total).astype(jnp.bfloat16)
+            if share >= BS:
+                each = share // BS
+                span = pl.ds(pl.multiple_of(block % each * BS, BS), BS)
+                results[phase, hop, block // each, span, :] = mixed
+            else:
+                each = BS // share
+                results[phase, hop, pl.ds(block * each, each)] = mixed.reshape(each, share, HD)
 
         def attend(phase):
             head = plan.head_of(me, phase)
@@ -183,9 +248,12 @@
 
                     lax.fori_loop(0, blocks // side, some, 0)
 
+                    for over in range(1, groups):
+                        back(phase, hop, over, head).start()
+
                     @pl.when(hop > 0)
                     def _():
-                        back(phase, hop, head).start()
+                        back(phase, hop, 0, head).start()
 
                     @pl.when(hop == 0)
                     def _():
@@ -195,12 +263,15 @@
 
             lax.fori_loop(0, count, one_home, 0)
 
-        greet(count)
+        greet(count, groups)
         for hop in range(1, count):
             small(hop).start()
         tables[0] = t_ref[...]
         for phase in range(min(2, phases)):
             send(phase)
+        for i in range(FETCHED):
+            for over in range(1, groups):
+                over_y(over, i).start()
         for hop in range(1, count):
             small(hop).wait()
         to_scalar = pltpu.make_async_copy(tables, lists, own.at[phases])
@@ -211,8 +282,13 @@
             arrive(phase)
             if phase + 2 < phases:
                 send(phase + 2)
+            if phase:
+                for i in range(FETCHED * (phase - 1) // (phases - 1), FETCHED * phase // (phases - 1)):
+                    pass_on(i)
             attend(phase)
 
+        for i in range(FETCHED, CHUNKS):
+            pass_on(i)
         for phase in range(phases):
             for hop in range(1, count):
                 big(phase, hop, True).wait_send()
@@ -225,31 +301,48 @@
 
                 @pl.when(plan.active((me + count - hop) % count, me, phase))
                 def _():
-                    if hop:
-                        back(phase, hop, plan.head_of(me, phase)).wait_send()
-                    else:
-                        stay(phase, plan.head_of(me, phase)).wait()
+                    for over in range(groups):
+                        if hop or over:
+                            back(phase, hop, over, plan.head_of(me, phase)).wait_send()
+                        else:
+                            stay(phase, plan.head_of(me, phase)).wait()
 
         for head in range(heads):
-
-            @pl.when(plan.handler(me, head) != me)
-            def _():
-                back(0, 1, head).wait_recv()
-
-            out_ref[:, head * HD : (head + 1) * HD] = landed[head]
+            for over in range(groups):
+                if over:
+                    back(0, 1, over, head).wait_recv()
+                else:
+
+                    @pl.when(plan.handler(me, head) != me)
+                    def _():
+                        back(0, 1, 0, head).wait_recv()
+
+                out_ref[over, :, head * HD : (head + 1) * HD] = landed[over, head]
+
+        for over in range(1, groups):
+            for i in range(CHUNKS):
+                if i < FETCHED:
+                    over_y(over, i).wait_send()
+                if i < CHUNKS - FETCHED:
+                    over_x(over, i).wait_send()
+                over_core(over, i).wait()
 
     vmem = pl.BlockSpec(memory_space=pltpu.VMEM)
+    any_spec = pl.BlockSpec(memory_space=pl.ANY)
     dma = pltpu.SemaphoreType.DMA
     kind = queries.dtype
     return pl.pallas_call(
         body,
-        out_shape=jax.ShapeDtypeStruct((rows, heads * HD), kind),
-        in_specs=[vmem] * 4,
-        out_specs=vmem,
+        out_shape=[
+            jax.ShapeDtypeStruct((groups, share, heads * HD), kind),
+            jax.ShapeDtypeStruct((groups - 1, *out_weight.shape), kind),
+        ],
+        in_specs=[vmem] * 4 + [any_spec],
+        out_specs=[vmem, any_spec],
         scratch_shapes=[
             pltpu.VMEM((phases, count, 3, blocks, BS, HD), kind),
-            pltpu.VMEM((phases, count, rows, HD), kind),
-            pltpu.VMEM((heads, rows, HD), kind),
+            pltpu.VMEM((phases, count, groups, share, HD), kind),
+            pltpu.VMEM((groups, heads, share, HD), kind),
             pltpu.VMEM((count, META, HD), jnp.int32),
             pltpu.SMEM((count, META, HD), jnp.int32),
             pltpu.VMEM((side, KB, BS, BS), jnp.float32),
@@ -257,9 +350,15 @@
             dma((phases, count, 2)),
             dma((count,)),
             dma((count,)),
-            dma((phases, count)),
-            dma((heads,)),
+            dma((phases, count, groups)),
+            dma((groups, heads)),
             dma((phases + 1,)),
+            dma((groups - 1, FETCHED)),
+            dma((groups - 1, FETCHED)),
+            dma((groups - 1, CHUNKS - FETCHED)),
+            dma((groups - 1, CHUNKS - FETCHED)),
+            dma((groups - 1, CHUNKS)),
+            dma((groups - 1, CHUNKS)),
         ]
         + [pltpu.VMEM((count, 3, blocks, BS, HD), kind)] * phases,
         compiler_params=pltpu.CompilerParams(
@@ -270,38 +369,19 @@
             bytes_accessed=8 * heads * rows * HD,
             transcendentals=heads * rows * BS * KB,
         ),
-    )(queries, keys, values, table)
-
-
-def project(attended, out_weight):
-    groups = lax.axis_size("head")
-    mine = lax.axis_index("head")
-    rows = attended.shape[0] // groups
-    width = out_weight.shape[1]
-    cuts = 4
-    piece = width // cuts
-
-    def share(owner, cut):
-        return jnp.dot(
-            lax.dynamic_slice_in_dim(attended, owner * rows, rows, 0),
-            out_weight[:, cut * piece : (cut + 1) * piece],
+    )(queries, keys, values, table, out_weight)
+
+
+def project(attended, out_weight, others):
+    total = 0.0
+    for over in range(attended.shape[0]):
+        part = jnp.dot(
+            attended[over],
+            others[over - 1] if over else out_weight,
             preferred_element_type=jnp.float32,
-        ).astype(jnp.bfloat16)
-
-    arrived = [
-        [
-            lax.ppermute(share(mine ^ hop, cut), "head", [(g, g ^ hop) for g in range(groups)])
-            for hop in range(1, groups)
-        ]
-        for cut in range(cuts)
-    ]
-    done = []
-    for cut in range(cuts):
-        total = share(mine, cut).astype(jnp.float32)
-        for part in arrived[cut]:
-            total = total + part.astype(jnp.float32)
-        done.append(total.astype(jnp.bfloat16))
-    return jnp.concatenate(done, axis=1)
+        )
+        total = total + part.astype(jnp.bfloat16).astype(jnp.float32)
+    return total.astype(jnp.bfloat16)
 
 
 def on_device(queries, keys, values, block_list, block_count, out_weight):
@@ -311,7 +391,8 @@
     blocks = rows // BS
     table = jnp.concatenate([block_list, block_count[:, None]], axis=1)
     table = jnp.pad(table, ((0, META - blocks), (0, HD - KB - 1)))
-    return project(attention(plan, queries, keys, values, table), out_weight)
+    attended, others = attention(plan, queries, keys, values, table, out_weight)
+    return project(attended, out_weight, others)
 
 
 def solution(mesh):

time: 345 us -> 374 us (1.084)
  Pallas kernels: 271 us -> 346 us
  waiting for transfers between devices: 27.9 us -> 0 us
  matrix products: 37.7 us -> 25.7 us
  starting transfers between devices: 4.18 us -> 0 us
    pallas_call x1, Pallas kernels: 271 us -> 346 us  [attention(): pl.pallas_call(body, out_shape=[jax.ShapeDtypeStruct((groups, share, head...]
    ppermute x4 -> x0, waiting for transfers between devices: 27.9 us -> none  [project(): lax.ppermute(share(mine ^ hop, cut), 'head', [(g, g ^ hop) for g in range...]
    dot_general x8 -> x2, matrix products: 37.7 us -> 25.7 us  [project(): jnp.dot(attended[over], others[over - 1] if over else out_weight, preferr...]
    ppermute x4 -> x0, starting transfers between devices: 4.18 us -> none  [project(): lax.ppermute(share(mine ^ hop, cut), 'head', [(g, g ^ hop) for g in range...]
  transfers between devices with their start and end apart: 4 -> 0, of which waited for: 4 -> 0; matrix products, arithmetic and copies ran while one was open for 8% -> 0% of each run, Pallas kernels for 0% -> 0%
where the time goes in v4:
time: 374 us
  Pallas kernels  346 us (93%)
  matrix products  25.7 us (7%)
    pallas_call x1, Pallas kernels, attention(): pl.pallas_call(body, out_shape=[jax.ShapeDtypeStruct((groups, share, head...  346 us
    dot_general x2, matrix products, project(): jnp.dot(attended[over], others[over - 1] if over else out_weight, preferr...  25.7 us

profile of v4, /device:TPU:10, one launch (start us, length us, event | category | flops | bytes accessed | tf_op | source)
XLA Modules:
  0.0 373.7 jit_solution(10849981085966549926)
XLA Ops:
  0.0 0.7 copy.7
  0.7 0.8 pad_add_fusion
  1.5 0.6 pad.4.t_ref
  2.1 345.9 %shard_map.64 = (bf16[2,256,2560]{2,1,0:T(8,128)(2,1)}, bf16[1,2560,5120]{2,1,0:T(8,128)(2,1)}) custom-call(bf16[512,2560]{1,0:T(8,128)(2,1)} %q_ref.1, bf16[512,2560]{1,0:T(8,128)(2,1)} %k_ref.1, bf16[512,2560]{1,0:T(8,128)(2,1)} %v_ref.1, s32[8,128]{1,0:T(8,128)} %pad.4.t_ref, bf16[2560,5120]{1,0:T(8,128)(2,1)} %w_ref.1), custom_call_target="tpu_custom_call" | custom-call | flops 10737418240 | bytes 10485760 | tf_op jit(solution)/shard_map/pallas_call | solution.py:334
  348.0 0.0 copy-start
  348.0 12.5 %fusion.14 = f32[256,5120]{1,0:T(8,128)S(1)} fusion(bf16[2560,5120]{1,0:T(8,128)(2,1)} %w_ref.1, bf16[2,256,2560]{2,1,0:T(8,128)(2,1)} %get-tuple-element.7), kind=kOutput, calls=%fused_computation.7 | convolution fusion | flops 6713507840 | bytes 32768000 | tf_op jit(solution)/shard_map/dot_general | solution.py:378
  360.5 0.0 copy-done
  360.5 13.1 %fusion.11 = bf16[256,5120]{1,0:T(8,128)(2,1)} fusion(f32[256,5120]{1,0:T(8,128)S(1)} %fusion.14, bf16[1,2560,5120]{2,1,0:T(8,128)(2,1)} %get-tuple-element.8, bf16[2,256,2560]{2,1,0:T(8,128)(2,1)S(1)} %copy-done), kind=kOutput, calls=%fused_computation.5 | convolution fusion | flops 6716129280 | bytes 35389440 | tf_op jit(solution)/shard_map/dot_general | solution.py:378
Async XLA Ops:
  348.0 12.6 %copy-start = (bf16[2,256,2560]{2,1,0:T(8,128)(2,1)S(1)}, bf16[2,256,2560]{2,1,0:T(8,128)(2,1)}, u32[]{:S(2)}) copy-start(bf16[2,256,2560]{2,1,0:T(8,128)(2,1)} %get-tuple-element.7) | copy-start | bytes 7864324

commit v5 on v3

--- a/solution.py
+++ b/solution.py
@@ -278,7 +278,7 @@
     mine = lax.axis_index("head")
     rows = attended.shape[0] // groups
     width = out_weight.shape[1]
-    cuts = 4
+    cuts = 8
     piece = width // cuts
 
     def share(owner, cut):

time: 345 us -> 341 us (0.988)
  waiting for transfers between devices: 27.9 us -> 4.39 us
  matrix products: 37.7 us -> 54.2 us
  starting transfers between devices: 4.18 us -> 8.5 us
    ppermute x4 -> x8, waiting for transfers between devices: 27.9 us -> 4.39 us  [project(): lax.ppermute(share(mine ^ hop, cut), 'head', [(g, g ^ hop) for g in range...]
    dot_general x8 -> x16, matrix products: 37.7 us -> 54.2 us  [share(): jnp.dot(lax.dynamic_slice_in_dim(attended, owner * rows, rows, 0), out_we...]
    ppermute x4 -> x8, starting transfers between devices: 4.18 us -> 8.5 us  [project(): lax.ppermute(share(mine ^ hop, cut), 'head', [(g, g ^ hop) for g in range...]
  transfers between devices with their start and end apart: 4 -> 8, of which waited for: 4 -> 2; matrix products, arithmetic and copies ran while one was open for 8% -> 13% of each run, Pallas kernels for 0% -> 0%
where the time goes in v5:
time: 341 us
  Pallas kernels  271 us (79%)
  matrix products  54.2 us (16%)
  starting transfers between devices  8.5 us (2%)
  waiting for transfers between devices  4.39 us (1%)
    pallas_call x1, Pallas kernels, attention(): pl.pallas_call(body, out_shape=jax.ShapeDtypeStruct((rows, heads * HD), k...  271 us
    dot_general x16, matrix products, share(): jnp.dot(lax.dynamic_slice_in_dim(attended, owner * rows, rows, 0), out_we...  54.2 us
    ppermute x8, starting transfers between devices, project(): lax.ppermute(share(mine ^ hop, cut), 'head', [(g, g ^ hop) for g in range...  8.5 us
  transfers between devices with their start and end apart: 8, of which 2 were waited for; matrix products, arithmetic and copies ran while one was open for 13% of the time, Pallas kernels for 0%

profile of v5, /device:TPU:10, one launch (start us, length us, event | category | flops | bytes accessed | tf_op | source)
XLA Modules:
  0.0 340.6 jit_solution(6656446152713232048)
XLA Ops:
  0.0 0.7 copy.7
  0.7 0.8 pad_add_fusion
  1.5 0.6 pad.4.t_ref
  2.1 271.3 %shard_map.64 = bf16[512,2560]{1,0:T(8,128)(2,1)} custom-call(bf16[512,2560]{1,0:T(8,128)(2,1)} %q_ref.1, bf16[512,2560]{1,0:T(8,128)(2,1)} %k_ref.1, bf16[512,2560]{1,0:T(8,128)(2,1)} %v_ref.1, s32[8,128]{1,0:T(8,128)} %pad.4.t_ref), custom_call_target="tpu_custom_call" | custom-call | flops 10737418240 | bytes 10485760 | tf_op jit(solution)/shard_map/pallas_call | solution.py:244
  273.4 4.4 %fusion.38 = bf16[256,640]{1,0:T(8,128)(2,1)} fusion(bf16[2560,5120]{1,0:T(8,128)(2,1)} %param.11, bf16[512,2560]{1,0:T(8,128)(2,1)} %shard_map.64, s32[]{:T(128)S(6)} %select_n.5), kind=kOutput, calls=%fused_computation.34 | convolution fusion | flops 839024640 | bytes 4915204 | tf_op jit(solution)/shard_map/dot_general | solution.py:285
  277.8 1.5 collective-permute-start
  279.3 3.8 %fusion.47 = bf16[256,640]{1,0:T(8,128)(2,1)} fusion(bf16[2560,5120]{1,0:T(8,128)(2,1)} %param.11, bf16[512,2560]{1,0:T(8,128)(2,1)S(1)} %copy-done, s32[]{:T(128)S(6)} %select_n.5), kind=kOutput, calls=%fused_computation.37 | convolution fusion | flops 839024640 | bytes 4915204 | tf_op jit(solution)/shard_map/dot_general | solution.py:285
  283.2 0.5 collective-permute-start.1
  283.7 3.1 fusion.56
  286.8 1.6 collective-permute-start.2
  288.4 3.1 fusion.65
  291.5 0.6 collective-permute-start.3
  292.1 3.1 fusion.74
  295.2 1.6 collective-permute-start.4
  296.7 3.7 %fusion.83 = bf16[256,640]{1,0:T(8,128)(2,1)S(1)} fusion(bf16[2560,5120]{1,0:T(8,128)(2,1)} %param.11, bf16[512,2560]{1,0:T(8,128)(2,1)} %shard_map.64, s32[]{:T(128)S(6)} %select_n.5), kind=kOutput, calls=%fused_computation.49 | convolution fusion | flops 839024640 | bytes 4915204 | tf_op jit(solution)/shard_map/dot_general | solution.py:285
  300.4 3.1 fusion.92
  303.6 3.7 %fusion.101 = bf16[256,640]{1,0:T(8,128)(2,1)S(1)} fusion(bf16[2560,5120]{1,0:T(8,128)(2,1)} %param.11, bf16[512,2560]{1,0:T(8,128)(2,1)} %shard_map.64, s32[]{:T(128)S(6)} %select_n.5), kind=kOutput, calls=%fused_computation.55 | convolution fusion | flops 839024640 | bytes 4915204 | tf_op jit(solution)/shard_map/dot_general | solution.py:285
  307.2 0.0 collective-permute-done
  307.2 0.6 collective-permute-start.5
  307.8 3.2 fusion.104
  311.1 1.6 collective-permute-start.6
  312.6 3.1 fusion.105
  315.8 0.6 collective-permute-start.7
  316.4 3.1 fusion.106
  319.5 3.1 fusion.107
  322.7 3.4 fusion.108
  326.1 3.1 fusion.109
  329.2 1.5 collective-permute-done.6
  330.7 3.2 fusion.110
  333.9 0.0 copy-start.3
  333.9 2.9 collective-permute-done.7
  336.8 3.8 %fusion.111 = bf16[256,5120]{1,0:T(8,128)(2,1)} fusion(bf16[256,5120]{1,0:T(8,128)(2,1)} %copy-done.3, bf16[256,640]{1,0:T(8,128)(2,1)S(1)} %collective-permute-done.7, bf16[2560,5120]{1,0:T(8,128)(2,1)} %param.11, bf16[512,2560]{1,0:T(8,128)(2,1)S(1)} %copy-done.2, s32[]{:T(128)S(6)} %select_n.4), kind=kOutput, calls=%fused_computation.71 | convolution fusion | flops 839680000 | bytes 5242884 | tf_op jit(solution)/shard_map/dot_general | solution.py:285
  (12 shorter events, 0.0 us)
Async XLA Ops:
  273.4 5.9 %copy-start = (bf16[512,2560]{1,0:T(8,128)(2,1)S(1)}, bf16[512,2560]{1,0:T(8,128)(2,1)}, u32[]{:S(2)}) copy-start(bf16[512,2560]{1,0:T(8,128)(2,1)} %shard_map.64) | copy-start | bytes 7864324
  277.8 29.4 %collective-permute-start = (bf16[256,640]{1,0:T(8,128)(2,1)}, bf16[256,640]{1,0:T(8,128)(2,1)S(1)}, u32[]{:S(2)}, u32[]{:S(2)}) collective-permute-start(bf16[256,640]{1,0:T(8,128)(2,1)} %fusion.38), channel_id=1, source_target_pairs={{0,1},{1,0},{2,3},{3,2},{4,5},{5,4},{6,7},{7,6},{8,9},{9,8},{10,11... | collective-permute-start | bytes 983048 | tf_op jit(solution)/shard_map/ppermute | solution.py:293
  283.2 27.9 %collective-permute-start.1 = (bf16[256,640]{1,0:T(8,128)(2,1)}, bf16[256,640]{1,0:T(8,128)(2,1)S(1)}, u32[]{:S(2)}, u32[]{:S(2)}) collective-permute-start(bf16[256,640]{1,0:T(8,128)(2,1)} %fusion.47), channel_id=1, source_target_pairs={{0,1},{1,0},{2,3},{3,2},{4,5},{5,4},{6,7},{7,6},{8,9},{9,8},{10,11... | collective-permute-start | bytes 983048 | tf_op jit(solution)/shard_map/ppermute | solution.py:293
  286.8 29.0 %collective-permute-start.2 = (bf16[256,640]{1,0:T(8,128)(2,1)S(1)}, bf16[256,640]{1,0:T(8,128)(2,1)S(1)}, u32[]{:S(2)}, u32[]{:S(2)}) collective-permute-start(bf16[256,640]{1,0:T(8,128)(2,1)S(1)} %fusion.56), channel_id=1, source_target_pairs={{0,1},{1,0},{2,3},{3,2},{4,5},{5,4},{6,7},{7,6},{8,9},{9,8},{10,11... | collective-permute-start | bytes 983048 | tf_op jit(solution)/shard_map/ppermute | solution.py:293
  291.5 28.0 %collective-permute-start.3 = (bf16[256,640]{1,0:T(8,128)(2,1)S(1)}, bf16[256,640]{1,0:T(8,128)(2,1)S(1)}, u32[]{:S(2)}, u32[]{:S(2)}) collective-permute-start(bf16[256,640]{1,0:T(8,128)(2,1)S(1)} %fusion.65), channel_id=1, source_target_pairs={{0,1},{1,0},{2,3},{3,2},{4,5},{5,4},{6,7},{7,6},{8,9},{9,8},{10,11... | collective-permute-start | bytes 983048 | tf_op jit(solution)/shard_map/ppermute | solution.py:293
  295.2 27.5 %collective-permute-start.4 = (bf16[256,640]{1,0:T(8,128)(2,1)S(1)}, bf16[256,640]{1,0:T(8,128)(2,1)S(1)}, u32[]{:S(2)}, u32[]{:S(2)}) collective-permute-start(bf16[256,640]{1,0:T(8,128)(2,1)S(1)} %fusion.74), channel_id=1, source_target_pairs={{0,1},{1,0},{2,3},{3,2},{4,5},{5,4},{6,7},{7,6},{8,9},{9,8},{10,11... | collective-permute-start | bytes 983048 | tf_op jit(solution)/shard_map/ppermute | solution.py:293
  296.7 3.7 %copy-start.1 = (bf16[512,2560]{1,0:T(8,128)(2,1)S(1)}, bf16[512,2560]{1,0:T(8,128)(2,1)}, u32[]{:S(2)}) copy-start(bf16[512,2560]{1,0:T(8,128)(2,1)} %shard_map.64) | copy-start | bytes 7864324
  303.6 4.3 %copy-start.2 = (bf16[512,2560]{1,0:T(8,128)(2,1)S(1)}, bf16[512,2560]{1,0:T(8,128)(2,1)}, u32[]{:S(2)}) copy-start(bf16[512,2560]{1,0:T(8,128)(2,1)} %shard_map.64) | copy-start | bytes 7864324
  307.2 18.8 %collective-permute-start.5 = (bf16[256,640]{1,0:T(8,128)(2,1)S(1)}, bf16[256,640]{1,0:T(8,128)(2,1)S(1)}, u32[]{:S(2)}, u32[]{:S(2)}) collective-permute-start(bf16[256,640]{1,0:T(8,128)(2,1)S(1)} %fusion.83), channel_id=1, source_target_pairs={{0,1},{1,0},{2,3},{3,2},{4,5},{5,4},{6,7},{7,6},{8,9},{9,8},{10,11... | collective-permute-start | bytes 983048 | tf_op jit(solution)/shard_map/ppermute | solution.py:293
  311.1 19.7 %collective-permute-start.6 = (bf16[256,640]{1,0:T(8,128)(2,1)S(1)}, bf16[256,640]{1,0:T(8,128)(2,1)S(1)}, u32[]{:S(2)}, u32[]{:S(2)}) collective-permute-start(bf16[256,640]{1,0:T(8,128)(2,1)S(1)} %fusion.92), channel_id=1, source_target_pairs={{0,1},{1,0},{2,3},{3,2},{4,5},{5,4},{6,7},{7,6},{8,9},{9,8},{10,11... | collective-permute-start | bytes 983048 | tf_op jit(solution)/shard_map/ppermute | solution.py:293
  315.8 21.0 %collective-permute-start.7 = (bf16[256,640]{1,0:T(8,128)(2,1)S(1)}, bf16[256,640]{1,0:T(8,128)(2,1)S(1)}, u32[]{:S(2)}, u32[]{:S(2)}) collective-permute-start(bf16[256,640]{1,0:T(8,128)(2,1)S(1)} %fusion.101), channel_id=1, source_target_pairs={{0,1},{1,0},{2,3},{3,2},{4,5},{5,4},{6,7},{7,6},{8,9},{9,8},{10,11... | collective-permute-start | bytes 983048 | tf_op jit(solution)/shard_map/ppermute | solution.py:293
  333.9 2.9 copy-start.3
